TPU v7x, 256 devices: a whole 4x4x8 slice. The times are simulated.
256 devices in a mesh: group: 16 (over y_hi, x, core), seq: 16 (over z, y_lo).
Axes of the slice: x: 4, y: 4 (y_hi: 2, y_lo: 2; y = y_hi * 2 + y_lo), z: 8, core: 2. Of those that a mesh axis runs over, the one named last changes fastest.
Arguments:
- latent: float32 [32, 1024, 64], P('group', 'seq'), may hold values from -6 to 6
- margin_len: int32 [31], replicated, may hold values from 1 to 512, 11904 in all
- in_weight: bfloat16 [64, 1536], replicated, may hold values from -0.75 to 0.75
- norm_gain: float32 [1536], replicated, may hold values from 0.1 to 1.9
- qkv_weight: bfloat16 [3, 1536, 1024], P(None, None, 'seq'), may hold values from -0.15625 to 0.15625
- out_weight: bfloat16 [1024, 1536], P('seq'), may hold values from -0.1875 to 0.1875
- final_gain: float32 [1536], replicated, may hold values from 0.1 to 1.9
- head_out: bfloat16 [1536, 64], replicated, may hold values from -0.15625 to 0.15625
Outputs:
- next_latent: float32 [32, 1024, 64], P('group', 'seq')
Inputs may be any that keep to these rules, and one draw needn't show every extreme that they name: `margin_len`: the lengths sum to 31 * (384) and the largest is exactly 512.
All inputs are finite; a program needn't handle non-finite values.
Results may differ from a plain program's by a relative error of at most 0.0024.
Values may be sent and summed in bfloat16 or wider, within the bound.
A program may use at most 128 MiB of HBM per device.

v0:
```python
import jax
import jax.numpy as jnp
from jax import lax
from jax.sharding import PartitionSpec as P

HDIM = 64
OVMAX = 512


STEP = -0.5


def shifted(value, axis, by):
    size = lax.axis_size(axis)
    pairs = [(i, i + by) for i in range(size) if 0 <= i + by < size]
    return lax.ppermute(value, axis, pairs)


def joined_along(parts, dim):
    shape = list(parts.shape[1:])
    shape[dim] *= parts.shape[0]
    return jnp.moveaxis(parts, 0, dim).reshape(shape)


def sent_to_all(value, axis):
    size = lax.axis_size(axis)
    return lax.all_to_all(
        jnp.broadcast_to(value[None], (size, *value.shape)), axis, 0, 0, tiled=True
    )


def gathered_copies(value, axis, dim):
    return joined_along(sent_to_all(value, axis), dim)


def split_up(value, dim, size):
    shape = value.shape
    parts = value.reshape(*shape[:dim], size, shape[dim] // size, *shape[dim + 1 :])
    return jnp.moveaxis(parts, dim, 0)


def sent_and_summed(value, axis, dim):
    parts = split_up(value, dim, lax.axis_size(axis))
    arrived = lax.all_to_all(parts, axis, split_axis=0, concat_axis=0, tiled=True)
    return arrived.sum(axis=0)


def layer_norm(values_in, gain):
    row_mean = jnp.mean(values_in, axis=-1, keepdims=True)
    centered = values_in - row_mean
    variance = jnp.mean(centered * centered, axis=-1, keepdims=True)
    return centered / jnp.sqrt(variance + 1e-05) * gain


def rms_heads(values_in):
    return values_in / jnp.sqrt(jnp.mean(values_in * values_in, axis=-1, keepdims=True) + 1e-06)


def local_heads(windows, key_counts, in_weight, norm_gain, qkv_part):
    tokens = windows.shape[0]
    inputs = jnp.einsum(
        "tnc,cd->tnd", windows.astype(jnp.bfloat16), in_weight, preferred_element_type=jnp.float32
    )
    normed = layer_norm(inputs, norm_gain).astype(jnp.bfloat16)
    local_width = qkv_part.shape[2]
    head_count = local_width // HDIM

    def project(which_part):
        projected = jnp.einsum(
            "tnd,de->tne", normed, qkv_part[which_part], preferred_element_type=jnp.float32
        )
        return projected.reshape(tokens, 2, head_count, HDIM)

    queries = rms_heads(project(0)).astype(jnp.bfloat16)
    keys_normed = rms_heads(project(1)).astype(jnp.bfloat16)
    values = project(2).astype(jnp.bfloat16)
    scores = jnp.einsum("qnhd,knhd->nhqk", queries, keys_normed, preferred_element_type=jnp.float32)
    key_mask = (jnp.arange(tokens)[None, :] < key_counts[:, None]).astype(jnp.float32)
    exp_scores = jnp.exp(scores * HDIM ** (-0.5)) * key_mask[:, None, None, :]
    weights = (exp_scores / jnp.sum(exp_scores, axis=-1, keepdims=True)).astype(jnp.bfloat16)
    attention = jnp.einsum("nhqk,knhd->qnhd", weights, values, preferred_element_type=jnp.float32)
    return (inputs, attention.astype(jnp.bfloat16).reshape(tokens, 2, local_width))


def body(latent, margin_len, in_weight, norm_gain, qkv_weight, out_weight, final_gain, head_out):
    seq_count = lax.axis_size("seq")
    group_pos = lax.axis_index("group")
    seq_pos = lax.axis_index("seq")
    slot_rows = latent.shape[1]
    group_len = slot_rows * seq_count
    lengths = jnp.concatenate([margin_len, jnp.zeros((1,), jnp.int32)])
    first_len = lengths[2 * group_pos]
    second_len = lengths[2 * group_pos + 1]
    following = shifted(latent[0], "group", -1)
    three_slots = jnp.stack([latent[0], latent[1], following])
    gathered = gathered_copies(three_slots.astype(jnp.bfloat16), "seq", 1).astype(three_slots.dtype)
    flat_rows = gathered.reshape(3 * group_len, gathered.shape[2])
    steps_t = jnp.arange(group_len, dtype=jnp.int32)

    def group_index(base_row, length):
        own_len = group_len - length
        return jnp.where(
            steps_t < own_len, base_row + steps_t, base_row + group_len + steps_t - own_len
        )

    group_rows = jnp.stack([group_index(0, first_len), group_index(group_len, second_len)], axis=1)
    spots = jnp.arange(OVMAX, dtype=jnp.int32)
    over_rows = jnp.stack([group_len + spots, 2 * group_len + spots], axis=1)
    group_win = jnp.take(flat_rows, group_rows, axis=0)
    over_win = jnp.take(flat_rows, over_rows, axis=0)
    group_counts = jnp.full((2,), group_len, jnp.int32)
    over_lens = jnp.stack([first_len, second_len])
    over_counts = jnp.maximum(over_lens, 1)
    group_in, group_att = local_heads(group_win, group_counts, in_weight, norm_gain, qkv_weight)
    over_in, over_att = local_heads(over_win, over_counts, in_weight, norm_gain, qkv_weight)
    group_share = group_len // seq_count
    second_share = over_att.shape[0] // seq_count
    full_out = lax.all_gather(out_weight, "seq", axis=0, tiled=True)
    group_mixed = lax.all_to_all(group_att, "seq", split_axis=0, concat_axis=2, tiled=True)
    over_mixed = lax.all_to_all(over_att, "seq", split_axis=0, concat_axis=2, tiled=True)
    group_proj = jnp.einsum(
        "tne,ed->tnd", group_mixed, full_out, preferred_element_type=jnp.float32
    )
    over_proj = jnp.einsum("tne,ed->tnd", over_mixed, full_out, preferred_element_type=jnp.float32)

    def finish(inputs, projected, share):
        own_inputs = lax.dynamic_slice_in_dim(inputs, seq_pos * share, share, 0)
        final_norm = layer_norm(own_inputs + projected, final_gain).astype(jnp.bfloat16)
        return jnp.einsum("tnd,dc->tnc", final_norm, head_out, preferred_element_type=jnp.float32)

    group_score = finish(group_in, group_proj, group_share)
    over_score = finish(over_in, over_proj, second_share)
    channels = group_score.shape[2]
    row_ids = seq_pos * slot_rows + jnp.arange(slot_rows, dtype=jnp.int32)
    group_target = lax.dynamic_slice_in_dim(group_rows, seq_pos * group_share, group_share, 0)
    over_target = lax.dynamic_slice_in_dim(over_rows, seq_pos * second_share, second_share, 0)
    over_tok = seq_pos * second_share + jnp.arange(second_share, dtype=jnp.int32)
    over_valid = (over_tok[:, None] < over_lens[None, :]).astype(jnp.float32)
    signed_over = -over_score * over_valid[:, :, None]
    target_rows = jnp.concatenate([group_target.reshape(-1), over_target.reshape(-1)])
    contrib_vals = jnp.concatenate(
        [group_score.reshape(-1, channels), signed_over.reshape(-1, channels)]
    )
    contrib = jnp.zeros((3 * group_len, channels), jnp.float32).at[target_rows].add(contrib_vals)
    contrib = contrib.reshape(3, group_len, channels)
    summed = sent_and_summed(contrib, "seq", 1)
    carried = shifted(summed[2], "group", 1)
    assembled = jnp.stack([summed[0] + carried, summed[1]])
    own_lens = jnp.stack([group_len - first_len, group_len - second_len])
    keep_rows = row_ids[None, :] < own_lens[:, None]
    return jnp.where(keep_rows[:, :, None], latent + STEP * assembled, jnp.float32(0.0))


def solution(mesh):
    in_specs = (
        P("group", "seq", None),
        P(),
        P(),
        P(),
        P(None, None, "seq"),
        P("seq", None),
        P(),
        P(),
    )
    out_specs = P("group", "seq", None)
    return jax.shard_map(body, mesh=mesh, in_specs=in_specs, out_specs=out_specs, check_vma=False)
```

profile of v0, /device:TPU:16, one launch (start us, length us, event | category | flops | bytes accessed | tf_op | source)
XLA Modules:
  0.0 177.6 jit_solution(4778457530577998559)
XLA Ops:
  7.3 3.9 %collective-permute-start = (bf16[64,64]{1,0:T(8,128)(2,1)S(1)}, bf16[64,64]{1,0:T(8,128)(2,1)S(1)}, u32[]{:S(2)}, u32[]{:S(2)}) collective-permute-start(bf16[64,64]{1,0:T(8,128)(2,1)S(1)} %slice_bitcast_fusion.2), channel_id=1, source_target_pairs={{16,0},{32,16},{48,32},{64,48},{80,64},{96,80},{112,96},{128,112},... | collective-permute-start | bytes 24584 | tf_op jit(solution)/shard_map/ppermute | solution.py:16
  19.2 10.2 %all-to-all-start = ((bf16[16,2,6144]{2,1,0:T(2,128)(2,1)}), bf16[16,2,6144]{2,1,0:T(2,128)(2,1)S(1)}, u32[]{:S(2)}, u32[]{:S(2)}) async-start(bf16[16,2,6144]{2,1,0:T(2,128)(2,1)} %reshape.618), calls=%async_computation | async-start | bytes 786432 | tf_op jit(solution)/shard_map/all_to_all | solution.py:27
  29.5 17.5 %all-to-all-done = bf16[16,2,6144]{2,1,0:T(2,128)(2,1)S(1)} async-done(((bf16[16,2,6144]{2,1,0:T(2,128)(2,1)}), bf16[16,2,6144]{2,1,0:T(2,128)(2,1)S(1)}, u32[]{:S(2)}, u32[]{:S(2)}) %all-to-all-start) | async-done | bytes 393248 | tf_op jit(solution)/shard_map/all_to_all | solution.py:27
  47.5 3.2 %gather_fusion.1 = bf16[1024,64]{1,0:T(8,128)(2,1)S(1)} fusion(bf16[3072,64]{1,0:T(8,128)(2,1)S(1)} %bitcast.132, s32[1024]{0:T(1024)S(1)} %broadcast_clamp_fusion.1), kind=kCustom, calls=%fused_computation.1 | custom fusion | bytes 266240 | tf_op jit(solution)/shard_map/jit(_take)/gather | solution.py:110
  58.3 6.2 %gather_fusion = bf16[2048,64]{1,0:T(8,128)(2,1)S(1)} fusion(bf16[3072,64]{1,0:T(8,128)(2,1)S(1)} %bitcast.133, s32[2048]{0:T(1024)S(1)} %broadcast_clamp_fusion), kind=kCustom, calls=%fused_computation | custom fusion | bytes 532480 | tf_op jit(solution)/shard_map/jit(_take)/gather | solution.py:109
  64.8 1.9 %fusion.79 = (f32[1024,2]{0,1:T(2,128)S(1)}, f32[1024,2,1536]{2,0,1:T(8,128)S(1)}) fusion(bf16[64,1536]{1,0:T(8,128)(2,1)S(1)} %copy-done, bf16[1024,2,64]{0,2,1:T(8,128)(2,1)S(1)} %copy.65, pred[1024,2]{0,1:T(4,128)(4,1)S(1)} %compare_and_fusion), kind=kOutput, calls=%fused_computation.152 | convolution fusion | flops 405927936 | bytes 13051904 | tf_op jit(solution)/shard_map/tnc,cd->tnd/dot_general | solution.py:61
  68.2 3.9 %copy-done.1 = f32[1024,2,1536]{2,0,1:T(8,128)} copy-done((f32[1024,2,1536]{2,0,1:T(8,128)}, f32[1024,2,1536]{2,0,1:T(8,128)S(1)}, u32[]{:S(2)}) %copy-start.1) | copy-done | bytes 12582936
  72.1 2.9 %fusion.12 = (f32[2,512]{1,0:T(2,128)S(1)}, f32[2,512,512]{1,2,0:T(8,128)}) fusion(f32[2,512]{1,0:T(2,128)S(1)} %compare_convert_fusion, f32[512,2,64]{0,2,1:T(8,128)} %get-tuple-element.14, f32[512,2]{0,1:T(2,128)S(1)} %add_sqrt_fusion.3, f32[512,2,64]{0,2,1:T(8,128)} %get-tuple-element.16, f32[512,2]{0,1:T(2,128)S(1)} %add_sqrt_fusion.4), kind=kOutput, calls=%fused_computation.19 | convolution fusion | flops 68942848 | bytes 2637824 | tf_op jit(solution)/shard_map/qnhd,knhd->nhqk/dot_general | solution.py:77
  75.0 3.1 %fusion.15 = bf16[512,2,64]{0,2,1:T(8,128)(2,1)S(1)} fusion(bf16[512,2,1536]{2,0,1:T(8,128)(2,1)S(1)} %copy-done.5, f32[2,512,512]{1,2,0:T(8,128)} %get-tuple-element.18, f32[2,512]{1,0:T(2,128)S(1)} %get-tuple-element.17, f32[2,512]{1,0:T(2,128)S(1)} %compare_convert_fusion, bf16[3,1536,64]{1,2,0:T(8,128)(2,1)} %param.12), kind=kOutput, calls=%fused_computation.26 | convolution fusion | flops 270663680 | bytes 5578752 | tf_op jit(solution)/shard_map/nhqk,knhd->qnhd/dot_general | solution.py:81
  79.2 3.7 %all-to-all-start.2 = ((bf16[16,2,2048]{2,1,0:T(2,128)(2,1)}), bf16[16,2,2048]{2,1,0:T(2,128)(2,1)S(1)}, u32[]{:S(2)}, u32[]{:S(2)}) async-start(bf16[16,2,2048]{2,1,0:T(2,128)(2,1)} %reshape.620), calls=%async_computation.2 | async-start | bytes 262144 | tf_op jit(solution)/shard_map/all_to_all | solution.py:120
  82.9 5.8 %multiply_convert_fusion = bf16[1024,2,1536]{2,0,1:T(8,128)(2,1)S(1)} fusion(f32[1024,2,1536]{2,0,1:T(8,128)} %copy-done.1, f32[1536]{0:T(1024)S(1)} %copy-done.10, f32[1024,2]{0,1:T(2,128)S(1)} %add_sqrt_fusion.2, f32[1024,2]{0,1:T(2,128)S(1)} %broadcast_multiply_fusion), kind=kLoop, calls=%fused_computation.3 | loop fusion | flops 12582912 | bytes 18896896 | tf_op jit(solution)/shard_map/convert_element_type | solution.py:64
  88.8 2.0 %multiply_reduce_fusion.3 = (f32[1024,2]{0,1:T(2,128)S(1)}, f32[1024,2,64]{0,2,1:T(8,128)S(1)}) fusion(bf16[1024,2,1536]{2,0,1:T(8,128)(2,1)S(1)} %multiply_convert_fusion, bf16[3,1536,64]{1,2,0:T(8,128)(2,1)S(1)} %copy-done.8), kind=kOutput, calls=%fused_computation.37 | convolution fusion | flops 402913280 | bytes 7020544 | tf_op jit(solution)/shard_map/tnd,de->tne/dot_general | solution.py:69
  90.8 2.0 %multiply_reduce_fusion.4 = (f32[1024,2]{0,1:T(2,128)S(1)}, f32[1024,2,64]{0,2,1:T(8,128)S(1)}) fusion(bf16[1024,2,1536]{2,0,1:T(8,128)(2,1)S(1)} %multiply_convert_fusion, bf16[3,1536,64]{1,2,0:T(8,128)(2,1)S(1)} %copy-done.8), kind=kOutput, calls=%fused_computation.39 | convolution fusion | flops 402913280 | bytes 7020544 | tf_op jit(solution)/shard_map/tnd,de->tne/dot_general | solution.py:69
  92.8 4.4 %fusion = (f32[2,1024]{1,0:T(2,128)S(1)}, f32[2,1024,1024]{1,2,0:T(8,128)}) fusion(f32[1024]{0:T(1024)S(1)} %fusion.65, f32[1024,2,64]{0,2,1:T(8,128)S(1)} %get-tuple-element.24, f32[1024,2]{0,1:T(2,128)S(1)} %add_sqrt_fusion, f32[1024,2,64]{0,2,1:T(8,128)S(1)} %get-tuple-element.26, f32[1024,2]{0,1:T(2,128)S(1)} %add_sqrt_fusion.1), kind=kOutput, calls=%fused_computation.7 | convolution fusion | flops 275249152 | bytes 9465856 | tf_op jit(solution)/shard_map/qnhd,knhd->nhqk/dot_general | solution.py:77
  97.2 8.8 %fusion.14 = bf16[1024,2,64]{0,2,1:T(8,128)(2,1)S(1)} fusion(f32[2,1024,1024]{1,2,0:T(8,128)} %get-tuple-element.28, f32[2,1024]{1,0:T(2,128)S(1)} %get-tuple-element.27, f32[1024]{0:T(1024)S(1)} %fusion.65, bf16[1024,2,1536]{2,0,1:T(8,128)(2,1)} %copy-done.3, bf16[3,1536,64]{1,2,0:T(8,128)(2,1)S(1)} %copy-done.8), kind=kOutput, calls=%fused_computation.23 | convolution fusion | flops 679739392 | bytes 15151104 | tf_op jit(solution)/shard_map/nhqk,knhd->qnhd/dot_general | solution.py:81
  107.6 7.9 %all-to-all-start.1 = ((bf16[16,2,4096]{2,1,0:T(2,128)(2,1)}), bf16[16,2,4096]{2,1,0:T(2,128)(2,1)S(1)}, u32[]{:S(2)}, u32[]{:S(2)}) async-start(bf16[16,2,4096]{2,1,0:T(2,128)(2,1)} %reshape.622), calls=%async_computation.1 | async-start | bytes 524288 | tf_op jit(solution)/shard_map/all_to_all | solution.py:119
  116.1 10.1 %all-to-all-done.1 = bf16[16,2,4096]{2,1,0:T(2,128)(2,1)S(1)} async-done(((bf16[16,2,4096]{2,1,0:T(2,128)(2,1)}), bf16[16,2,4096]{2,1,0:T(2,128)(2,1)S(1)}, u32[]{:S(2)}, u32[]{:S(2)}) %all-to-all-start.1) | async-done | bytes 262176 | tf_op jit(solution)/shard_map/all_to_all | solution.py:119
  127.3 2.9 %fusion.80 = (f32[64,2]{0,1:T(2,128)S(1)}, f32[64,2,1536]{2,0,1:T(8,128)S(1)}) fusion(bf16[64,2,1024]{2,0,1:T(8,128)(2,1)S(1)} %all_to_all.36, bf16[1024,1536]{1,0:T(8,128)(2,1)} %all-gather.2.cloned.1.call-done, f32[1024,2,1536]{2,0,1:T(8,128)} %copy-done.1, s32[]{:T(128)S(6)} %select_n.117), kind=kOutput, calls=%fused_computation.153 | convolution fusion | flops 403046272 | bytes 4981252 | tf_op jit(solution)/shard_map/tne,ed->tnd/dot_general | solution.py:121
  134.9 1.9 %reshape.624 = f32[16,1,12288]{2,1,0:T(1,128)} reshape(f32[16,3,64,64]{3,2,1,0:T(8,128)S(1)} %copy.78) | data formatting | bytes 1572864
  136.8 3.8 %all-to-all-start.3 = ((f32[16,1,12288]{2,1,0:T(1,128)}), f32[16,1,12288]{2,1,0:T(1,128)S(1)}, u32[]{:S(2)}, u32[]{:S(2)}) async-start(f32[16,1,12288]{2,1,0:T(1,128)} %reshape.624), calls=%async_computation.3 | async-start | bytes 1572864 | tf_op jit(solution)/shard_map/all_to_all | solution.py:44
  140.7 16.6 %all-to-all-done.3 = f32[16,1,12288]{2,1,0:T(1,128)S(1)} async-done(((f32[16,1,12288]{2,1,0:T(1,128)}), f32[16,1,12288]{2,1,0:T(1,128)S(1)}, u32[]{:S(2)}, u32[]{:S(2)}) %all-to-all-start.3) | async-done | bytes 786464 | tf_op jit(solution)/shard_map/all_to_all | solution.py:44
  157.9 2.5 %reduce.12 = f32[16,12288]{1,0:T(8,128)S(1)} reduce(f32[16,1,12288]{2,1,0:T(1,128)S(1)} %all-to-all-done.3, f32[]{:T(128)} %broadcast.502), dimensions={1}, to_apply=%all_to_all.41.reduce_sub_computation | reduce | bytes 1572868 | tf_op jit(solution)/shard_map/all_to_all | solution.py:44
  161.2 1.9 %collective-permute-start.1 = (f32[64,64]{1,0:T(8,128)S(1)}, f32[64,64]{1,0:T(8,128)S(1)}, u32[]{:S(2)}, u32[]{:S(2)}) collective-permute-start(f32[64,64]{1,0:T(8,128)S(1)} %get-tuple-element.7), channel_id=1, source_target_pairs={{0,16},{16,32},{32,48},{48,64},{64,80},{80,96},{96,112},{112,128},... | collective-permute-start | bytes 49160 | tf_op jit(solution)/shard_map/ppermute | solution.py:16
  163.2 6.8 %collective-permute-done.1 = f32[64,64]{1,0:T(8,128)S(1)} collective-permute-done((f32[64,64]{1,0:T(8,128)S(1)}, f32[64,64]{1,0:T(8,128)S(1)}, u32[]{:S(2)}, u32[]{:S(2)}) %collective-permute-start.1) | collective-permute-done | bytes 16416 | tf_op jit(solution)/shard_map/ppermute | solution.py:16
  (116 shorter events, 28.4 us)
Async XLA Ops:
  6.5 44.4 %copy-start = (bf16[64,1536]{1,0:T(8,128)(2,1)S(1)}, bf16[64,1536]{1,0:T(8,128)(2,1)}, u32[]{:S(2)}) copy-start(bf16[64,1536]{1,0:T(8,128)(2,1)} %param.10) | copy-start | bytes 589828
  6.5 120.7 %all-gather.2.cloned.1.call-start = ((), (), s32[]{:S(2)}) async-start(), calls=%async_computation.4 | async-start | bytes 3342336 | tf_op jit(solution)/shard_map/all_gather | solution.py:118
  7.3 10.4 %collective-permute-start = (bf16[64,64]{1,0:T(8,128)(2,1)S(1)}, bf16[64,64]{1,0:T(8,128)(2,1)S(1)}, u32[]{:S(2)}, u32[]{:S(2)}) collective-permute-start(bf16[64,64]{1,0:T(8,128)(2,1)S(1)} %slice_bitcast_fusion.2), channel_id=1, source_target_pairs={{16,0},{32,16},{48,32},{64,48},{80,64},{96,80},{112,96},{128,112},... | collective-permute-start | bytes 24584 | tf_op jit(solution)/shard_map/ppermute | solution.py:16
  19.2 27.7 %all-to-all-start = ((bf16[16,2,6144]{2,1,0:T(2,128)(2,1)}), bf16[16,2,6144]{2,1,0:T(2,128)(2,1)S(1)}, u32[]{:S(2)}, u32[]{:S(2)}) async-start(bf16[16,2,6144]{2,1,0:T(2,128)(2,1)} %reshape.618), calls=%async_computation | async-start | bytes 786432 | tf_op jit(solution)/shard_map/all_to_all | solution.py:27
  50.9 1.9 %copy-start.10 = (f32[1536]{0:T(1024)S(1)}, f32[1536]{0:T(1024)}, u32[]{:S(2)}) copy-start(f32[1536]{0:T(1024)} %param.11) | copy-start | bytes 18436
  52.0 2.7 %copy-start.2 = (f32[512,2,1536]{2,0,1:T(8,128)}, f32[512,2,1536]{2,0,1:T(8,128)S(1)}, u32[]{:S(2)}) copy-start(f32[512,2,1536]{2,0,1:T(8,128)S(1)} %get-tuple-element.12) | copy-start | bytes 18874372
  52.8 1.9 %copy-start.7 = (bf16[3,1536,64]{1,2,0:T(8,128)(2,1)S(1)}, bf16[3,1536,64]{1,2,0:T(8,128)(2,1)}, u32[]{:S(2)}) copy-start(bf16[3,1536,64]{1,2,0:T(8,128)(2,1)} %param.12) | copy-start | bytes 1769476
  54.7 1.8 %copy-start.4 = (bf16[512,2,1536]{2,0,1:T(8,128)(2,1)}, bf16[512,2,1536]{2,0,1:T(8,128)(2,1)S(1)}, u32[]{:S(2)}) copy-start(bf16[512,2,1536]{2,0,1:T(8,128)(2,1)S(1)} %multiply_convert_fusion.1) | copy-start | bytes 9437188
  66.7 5.4 %copy-start.1 = (f32[1024,2,1536]{2,0,1:T(8,128)}, f32[1024,2,1536]{2,0,1:T(8,128)S(1)}, u32[]{:S(2)}) copy-start(f32[1024,2,1536]{2,0,1:T(8,128)S(1)} %get-tuple-element.22) | copy-start | bytes 37748740
  66.8 8.2 %copy-start.5 = (bf16[512,2,1536]{2,0,1:T(8,128)(2,1)S(1)}, bf16[512,2,1536]{2,0,1:T(8,128)(2,1)}, u32[]{:S(2)}) copy-start(bf16[512,2,1536]{2,0,1:T(8,128)(2,1)} %copy-done.4) | copy-start | bytes 9437188
  79.2 28.4 %all-to-all-start.2 = ((bf16[16,2,2048]{2,1,0:T(2,128)(2,1)}), bf16[16,2,2048]{2,1,0:T(2,128)(2,1)S(1)}, u32[]{:S(2)}, u32[]{:S(2)}) async-start(bf16[16,2,2048]{2,1,0:T(2,128)(2,1)} %reshape.620), calls=%async_computation.2 | async-start | bytes 262144 | tf_op jit(solution)/shard_map/all_to_all | solution.py:120
  82.9 5.9 %copy-start.8 = (bf16[3,1536,64]{1,2,0:T(8,128)(2,1)S(1)}, bf16[3,1536,64]{1,2,0:T(8,128)(2,1)}, u32[]{:S(2)}) copy-start(bf16[3,1536,64]{1,2,0:T(8,128)(2,1)} %param.12) | copy-start | bytes 1769476
  88.8 4.1 %copy-start.3 = (bf16[1024,2,1536]{2,0,1:T(8,128)(2,1)}, bf16[1024,2,1536]{2,0,1:T(8,128)(2,1)S(1)}, u32[]{:S(2)}) copy-start(bf16[1024,2,1536]{2,0,1:T(8,128)(2,1)S(1)} %multiply_convert_fusion) | copy-start | bytes 18874372
  106.4 24.0 %copy-start.11 = (bf16[1536,64]{0,1:T(8,128)(2,1)S(1)}, bf16[1536,64]{0,1:T(8,128)(2,1)}, u32[]{:S(2)}) copy-start(bf16[1536,64]{0,1:T(8,128)(2,1)} %param.15) | copy-start | bytes 589828
  106.4 24.0 %copy-start.12 = (f32[1536]{0:T(1024)S(1)}, f32[1536]{0:T(1024)}, u32[]{:S(2)}) copy-start(f32[1536]{0:T(1024)} %param.14) | copy-start | bytes 18436
  107.6 18.6 %all-to-all-start.1 = ((bf16[16,2,4096]{2,1,0:T(2,128)(2,1)}), bf16[16,2,4096]{2,1,0:T(2,128)(2,1)S(1)}, u32[]{:S(2)}, u32[]{:S(2)}) async-start(bf16[16,2,4096]{2,1,0:T(2,128)(2,1)} %reshape.622), calls=%async_computation.1 | async-start | bytes 524288 | tf_op jit(solution)/shard_map/all_to_all | solution.py:119
  127.3 3.6 %copy-start.6 = (bf16[1024,1536]{1,0:T(8,128)(2,1)S(1)}, bf16[1024,1536]{1,0:T(8,128)(2,1)}, u32[]{:S(2)}) copy-start(bf16[1024,1536]{1,0:T(8,128)(2,1)} %all-gather.2.cloned.1.call-done) | copy-start | bytes 9437188
  134.8 35.3 %copy-start.9 = (f32[2,64,64]{2,1,0:T(8,128)S(1)}, f32[2,64,64]{2,1,0:T(8,128)}, u32[]{:S(2)}) copy-start(f32[2,64,64]{2,1,0:T(8,128)} %param.8) | copy-start | bytes 98308
  136.8 20.6 %all-to-all-start.3 = ((f32[16,1,12288]{2,1,0:T(1,128)}), f32[16,1,12288]{2,1,0:T(1,128)S(1)}, u32[]{:S(2)}, u32[]{:S(2)}) async-start(f32[16,1,12288]{2,1,0:T(1,128)} %reshape.624), calls=%async_computation.3 | async-start | bytes 1572864 | tf_op jit(solution)/shard_map/all_to_all | solution.py:44
  161.2 8.8 %collective-permute-start.1 = (f32[64,64]{1,0:T(8,128)S(1)}, f32[64,64]{1,0:T(8,128)S(1)}, u32[]{:S(2)}, u32[]{:S(2)}) collective-permute-start(f32[64,64]{1,0:T(8,128)S(1)} %get-tuple-element.7), channel_id=1, source_target_pairs={{0,16},{16,32},{32,48},{48,64},{64,80},{80,96},{96,112},{112,128},... | collective-permute-start | bytes 49160 | tf_op jit(solution)/shard_map/ppermute | solution.py:16
Sparse Core Ops, SparseCore 0:
  11.4 87.5 all-gather.1
where the time goes:
time: 178 us
  waiting for transfers between devices  51.1 us (29%)
  matrix products  35 us (20%)
  starting transfers between devices  31.4 us (18%)
  local copies, waits for them, and re-layouts  26.8 us (15%)
  other arithmetic  18 us (10%)
  between operations  15.3 us (9%)
    all_to_all x1, waiting for transfers between devices, sent_to_all(): lax.all_to_all(jnp.broadcast_to(value[None], (size, *value.shape)), axis,...  17.5 us
    all_to_all x1, waiting for transfers between devices, sent_and_summed(): lax.all_to_all(parts, axis, split_axis=0, concat_axis=0, tiled=True)  16.6 us
    dot_general x2, matrix products, local_heads(): jnp.einsum('nhqk,knhd->qnhd', weights, values, preferred_element_type=jnp...  11.9 us
    unnamed x35, local copies, waits for them, and re-layouts  11.7 us
    all_to_all x1, starting transfers between devices, sent_to_all(): lax.all_to_all(jnp.broadcast_to(value[None], (size, *value.shape)), axis,...  10.2 us
    all_to_all x1, waiting for transfers between devices, body(): lax.all_to_all(group_att, 'seq', split_axis=0, concat_axis=2, tiled=True)  10.1 us
    all_to_all x1, starting transfers between devices, body(): lax.all_to_all(group_att, 'seq', split_axis=0, concat_axis=2, tiled=True)  7.86 us
    dot_general x4, matrix products, project(): jnp.einsum('tnd,de->tne', normed, qkv_part[which_part], preferred_element...  7.61 us
  transfers between devices with their start and end apart: 7, of which 4 were waited for; matrix products, arithmetic and copies ran while one was open for 34% of the time, Pallas kernels for 0%

commit v1 on v0

v1 whole, which is shorter than its diff:
```python
import functools
import math

import jax
import jax.numpy as jnp
from jax import lax
from jax.experimental import pallas as pl
from jax.experimental.pallas import tpu as pltpu
from jax.sharding import PartitionSpec as P

MESH = pl.DeviceIdType.MESH
BF = jnp.bfloat16
F32 = jnp.float32

HDIM = 64
STEP = -0.5
ROWS = 64
PACK = 32
QSCALE = HDIM**-0.5 * math.log2(math.e)


def dot(a, b):
    return jnp.dot(a, b, preferred_element_type=F32)


def dot_nt(a, b):
    return lax.dot_general(a, b, (((1,), (1,)), ((), ())), preferred_element_type=F32)


def hi_lo(x):
    hi = x.astype(BF)
    return hi, (x - hi.astype(F32)).astype(BF)


def packed(x):
    return jnp.concatenate([x[:PACK], x[PACK:]], axis=1)


def unpacked(x):
    return jnp.concatenate([x[:, :HDIM], x[:, HDIM:]], axis=0)


def reversal():
    r = lax.broadcasted_iota(jnp.int32, (ROWS, ROWS), 0)
    c = lax.broadcasted_iota(jnp.int32, (ROWS, ROWS), 1)
    return (r + c == ROWS - 1).astype(F32)


def kernel(
    groups,
    lat_ref,
    lens_ref,
    wi_ref,
    gain_ref,
    qkv_hbm,
    o_hbm,
    fgain_ref,
    ho_hbm,
    out_ref,
    qkv_v,
    o_v,
    ho_v,
    lat_send,
    lat_buf,
    fold_buf,
    mo_buf,
    xkt,
    w_head,
    w_tail,
    att,
    sc_send,
    sc_recv,
    load_sem,
    lat_ssem,
    lat_rsem,
    fold_ssem,
    fold_rsem,
    z_ssem,
    y_ssem,
    sib_ssem,
    mo_rsem,
    sc_ssem,
    sc_rsem,
):
    g = lax.axis_index("group")
    s = lax.axis_index("seq")
    z = s // 2
    y = s % 2
    core = g % 2
    prev_g = (g + groups - 1) % groups
    next_g = (g + 1) % groups
    sib_g = g + 1 - 2 * core
    y_g = (g + core * (groups // 2)) % groups
    y_s = 2 * z + 1 - y
    low = s < 8
    half = mo_buf.shape[2]

    loads = [
        pltpu.make_async_copy(qkv_hbm, qkv_v, load_sem.at[0]),
        pltpu.make_async_copy(o_hbm, o_v, load_sem.at[1]),
        pltpu.make_async_copy(ho_hbm, ho_v, load_sem.at[2]),
    ]
    for load in loads:
        load.start()

    barrier = pltpu.get_barrier_semaphore()

    def greet(gg, ss):
        pl.semaphore_signal(barrier, inc=1, device_id=(gg, ss), device_id_type=MESH)

    @pl.loop(1, 16)
    def _(k):
        greet(g, (s + k) % 16)

    @pl.when(low)
    def _():
        @pl.loop(0, 8)
        def _(k):
            greet(prev_g, 2 * k + 1)

    @pl.when(y == 1)
    def _():
        @pl.loop(0, 8)
        def _(k):
            greet(next_g, k)

    greet(sib_g, s)

    @pl.when(core == 1)
    def _():
        greet(y_g, y_s)

    flip = reversal().astype(BF)
    main_at = jnp.where(low, s, 31 - s)
    for a in range(2):
        rows = lat_ref[a].astype(BF)
        turned = jnp.where(low, rows.astype(F32), dot(flip, rows))
        lat_send[a] = packed(turned).astype(BF)

    n_greet = 16 + jnp.where(low, 8, 0) + jnp.where(y == 1, 8, 0) + core
    pl.semaphore_wait(barrier, n_greet)

    def lat_copy(which, a, k, gg, ss, at):
        return pltpu.make_async_remote_copy(
            src_ref=lat_send.at[a],
            dst_ref=lat_buf.at[at],
            send_sem=lat_ssem.at[which, k],
            recv_sem=lat_rsem.at[at],
            device_id=(gg, ss),
            device_id_type=MESH,
        )

    def lat_sends(act):
        @pl.loop(0, 8)
        def _(j):
            k = (z + j) % 8
            for a in range(2):

                @pl.when(jnp.logical_or(j != 0, y != a))
                def _():
                    act(lat_copy(a, a, j, g, 2 * k + a, main_at))

            @pl.when(low)
            def _():
                @pl.when(jnp.logical_or(j != 0, y != 0))
                def _():
                    act(lat_copy(2, 1, j, g, 2 * k, 8 + s))

                act(lat_copy(3, 0, j, prev_g, 2 * k + 1, 8 + s))

    lat_sends(lambda c: c.start())
    lat_buf[main_at] = lat_send[y]

    @pl.when(jnp.logical_and(low, y == 0))
    def _():
        lat_buf[8 + s] = lat_send[1]

    wi = wi_ref[...].astype(F32)
    centred = wi - jnp.mean(wi, axis=1, keepdims=True)
    wg_hi, wg_lo = hi_lo(centred * gain_ref[...])
    wg = jnp.concatenate([wg_hi, wg_lo], axis=0)
    loads[0].wait()
    wqkv = jnp.concatenate([qkv_v[0], qkv_v[1], qkv_v[2]], axis=1)
    fold2 = dot(wg, wqkv)
    fold = fold2[:64] + fold2[64:]
    qk = jnp.concatenate([fold[:, :64], fold[:, 64:128]], axis=0)
    fold_buf[pl.ds(pl.multiple_of(s * 64, 64), 64), :] = qk.T.astype(BF)

    def fold_copy(k, ss, block):
        rows = pl.ds(pl.multiple_of(block * 64, 64), 64)
        return pltpu.make_async_remote_copy(
            src_ref=fold_buf.at[rows],
            dst_ref=fold_buf.at[rows],
            send_sem=fold_ssem.at[k],
            recv_sem=fold_rsem.at[block],
            device_id=(g, ss),
            device_id_type=MESH,
        )

    @pl.loop(1, 16)
    def _(k):
        fold_copy(k, (s + k) % 16, s).start()

    mv_hi, mv_lo = hi_lo(fold[:, 128:])
    loads[1].wait()
    mo = dot(mv_hi, o_v[...]) + dot(mv_lo, o_v[...])

    def mo_rows(block):
        return pl.ds(pl.multiple_of(block * 64, 64), 64)

    mo_buf[0, mo_rows(s), :] = mo[:, :half].astype(BF)
    mo_buf[1, mo_rows(s), :] = mo[:, half:].astype(BF)

    def mo_copy(part, block, ssem, gg, ss):
        return pltpu.make_async_remote_copy(
            src_ref=mo_buf.at[part, mo_rows(block)],
            dst_ref=mo_buf.at[part, mo_rows(block)],
            send_sem=ssem,
            recv_sem=mo_rsem.at[part, block],
            device_id=(gg, ss),
            device_id_type=MESH,
        )

    ahead = 1 - 2 * core

    def far(t):
        return 2 * ((z - ahead * t + 8) % 8) + y

    def near(t):
        return 2 * ((z + ahead * t + 8) % 8) + y

    z_next = 2 * ((z + ahead + 8) % 8) + y
    z_back = 2 * ((z - ahead + 8) % 8) + y

    def other(block):
        return block + 1 - 2 * y

    def ring_far(t):
        return mo_copy(core, far(t), z_ssem.at[0, t], g, z_next)

    def ring_near(t):
        return mo_copy(core, near(t), z_ssem.at[1, t], g, z_back)

    def across(block):
        return mo_copy(core, block, y_ssem.at[block // 2], y_g, y_s)

    def to_sib(block):
        return mo_copy(core, block, sib_ssem.at[block], sib_g, s)

    ring_far(0).start()
    ring_near(0).start()
    across(s).start()

    c_hi, c_lo = hi_lo(centred)
    cc = jnp.concatenate([c_hi, c_lo], axis=0)
    gram4 = dot_nt(cc, cc)
    gram2 = gram4[:64] + gram4[64:]
    gram = (gram2[:, :64] + gram2[:, 64:]) * (1.0 / wi.shape[1])
    gram_hi, gram_lo = hi_lo(gram)
    gram_st = jnp.concatenate([gram_hi, gram_lo], axis=0)

    def variance(xt):
        gx = dot(gram_st, xt.astype(BF))
        return jnp.maximum(jnp.sum((gx[:64] + gx[64:]) * xt, axis=0, keepdims=True), 0.0)

    node = 2 * g + y
    tail_len = jnp.where(node < lens_ref.shape[0], lens_ref[jnp.minimum(node, lens_ref.shape[0] - 1)], 0)

    @pl.loop(0, 8)
    def _(k):
        @pl.when(k != s)
        def _():
            lat_copy(0, 0, 0, g, s, k).wait_recv()

        @pl.when(jnp.logical_or(k != s, y != 0))
        def _():
            lat_copy(0, 0, 0, g, s, 8 + k).wait_recv()

        @pl.when(15 - k != s)
        def _():
            lat_copy(0, 0, 0, g, s, 16 + k).wait_recv()

    line = lax.broadcasted_iota(jnp.int32, (256, 128), 0)
    lane = lax.broadcasted_iota(jnp.int32, (256, 128), 1)
    spot = 64 * (line // 32) + line % 32 + 32 * (lane // 64)
    head_lines = lat_buf[0:8].astype(F32).reshape(256, 128)
    tail_lines = jnp.where(
        spot < tail_len,
        lat_buf[8:16].astype(F32).reshape(256, 128),
        lat_buf[16:24].astype(F32).reshape(256, 128),
    )
    tokens = jnp.concatenate([unpacked(head_lines), unpacked(tail_lines)], axis=0)
    xt = tokens.T
    xkt[0:64, :] = jnp.zeros((64, 1024), BF)
    xkt[64:128, :] = xt.astype(BF)
    var = variance(xt)
    key_eps = 1e-6 * (var + 1e-5)
    scaled = xt * lax.rsqrt(var + 1e-5)
    extra = (lax.broadcasted_iota(jnp.int32, (64, 1024), 0) == 0).astype(F32)
    w = jnp.concatenate([scaled, extra], axis=0).T
    w_head[...] = w[:512].astype(BF)
    place = lax.broadcasted_iota(jnp.int32, (512, 128), 0)
    tail_spot = 64 * ((place % 256) // 32) + place % 32 + 32 * (place // 256)
    w_tail[:, :128] = w[512:].astype(BF)
    w_tail[:, 128:] = jnp.where(tail_spot < tail_len, w[512:], 0.0).astype(BF)

    q_line = lax.broadcasted_iota(jnp.int32, (32, 128), 0)
    q_lane = lax.broadcasted_iota(jnp.int32, (32, 128), 1)
    q_spot = 64 * z + q_line + 32 * (q_lane // 64)
    q_tail = jnp.where(q_spot < tail_len, lat_buf[8 + z].astype(F32), lat_buf[16 + z].astype(F32))
    q_tok = jnp.concatenate([unpacked(lat_buf[z].astype(F32)), unpacked(q_tail)], axis=0)
    q_xt = q_tok.T
    q_eps = 1e-6 * (variance(q_xt) + 1e-5)
    q_xtz = jnp.concatenate([q_xt.astype(BF), jnp.zeros((64, 128), BF)], axis=0)
    q_side = lax.broadcasted_iota(jnp.int32, (128, 128), 1) < 64

    def rms(x, eps, scale):
        parts = []
        for h in range(2):
            rows = x[64 * h : 64 * h + 64]
            mean = jnp.sum(rows * rows, axis=0, keepdims=True) * (1.0 / HDIM)
            parts.append(rows * (lax.rsqrt(mean + eps) * scale))
        return jnp.concatenate(parts, axis=0)

    @pl.loop(0, 8)
    def _(n):
        off = jnp.where(n % 2 == 1, (n + 1) // 2, 8 - n // 2)
        zz = (z + off) % 8
        for h in range(2):

            @pl.when(2 * zz + h != s)
            def _():
                fold_copy(0, s, 2 * zz + h).wait_recv()

        pair = fold_buf[pl.ds(pl.multiple_of(zz * 128, 128), 128), :]
        keys_t = rms(dot(pair, xkt[...]), key_eps, 1.0).astype(BF)
        query = rms(dot(pair, q_xtz), q_eps, QSCALE).T
        query2 = jnp.concatenate(
            [jnp.where(q_side, query, 0.0), jnp.where(q_side, 0.0, query)], axis=0
        ).astype(BF)
        p = jnp.exp2(dot(query2, keys_t)).astype(BF)
        u_head = dot(p[:, :512], w_head[...])
        u_tail = dot(p[:, 512:], w_tail[...])
        u_all = u_head + u_tail[:, :128]
        ratio = u_all[:, :64] / u_all[:, 64:65]
        u_over = jnp.concatenate([u_tail[64:128, 128:], u_tail[192:256, 128:]], axis=0)
        total = u_over[:, 64:65]
        over = u_over[:, :64] / jnp.where(total == 0.0, 1.0, total)
        columns = pl.ds(pl.multiple_of(zz * 128, 128), 128)
        att[0:128, columns] = jnp.concatenate([ratio[:128], ratio[128:]], axis=1).astype(BF)
        att[128:192, columns] = jnp.concatenate([over[:64], over[64:]], axis=1).astype(BF)

        t = (n + 1) // 2

        @pl.when(n % 2 == 1)
        def _():
            mo_copy(core, far(t), z_ssem.at[0, 0], g, s).wait_recv()

            @pl.when(t < 4)
            def _():
                ring_far(t).start()
                mo_copy(core, near(t), z_ssem.at[0, 0], g, s).wait_recv()

                @pl.when(t < 3)
                def _():
                    ring_near(t).start()

                across(near(t)).start()
                to_sib(near(t)).start()

            across(far(t)).start()
            to_sib(far(t)).start()

            mo_copy(core, other(far(t - 1)), z_ssem.at[0, 0], g, s).wait_recv()
            to_sib(other(far(t - 1))).start()

            @pl.when(t > 1)
            def _():
                mo_copy(core, other(near(t - 1)), z_ssem.at[0, 0], g, s).wait_recv()
                to_sib(other(near(t - 1))).start()

    last = other(far(4))
    mo_copy(core, last, z_ssem.at[0, 0], g, s).wait_recv()
    to_sib(last).start()

    @pl.loop(1, 16)
    def _(k):
        mo_copy(1 - core, (s + k) % 16, z_ssem.at[0, 0], g, s).wait_recv()

    tok2 = jnp.concatenate([q_tok, q_tok[64:]], axis=0).astype(BF)
    mixed = jnp.concatenate(
        [
            dot(att[...], mo_buf[k]) + dot(tok2, wi_ref[:, k * half : (k + 1) * half])
            for k in range(2)
        ],
        axis=1,
    )
    mean = jnp.mean(mixed, axis=1, keepdims=True)
    centre = mixed - mean
    spread = jnp.mean(centre * centre, axis=1, keepdims=True)
    loads[2].wait()
    final = (centre * lax.rsqrt(spread + 1e-5) * fgain_ref[...]).astype(BF)
    score = dot(final, ho_v[...])

    where_t = 64 * z + lax.broadcasted_iota(jnp.int32, (64, 64), 0)
    counted = where_t < tail_len
    sc_send[0] = score[:64]
    sc_send[1] = jnp.where(counted, score[64:128] - score[128:], 0.0)
    sc_send[2] = jnp.dot(
        reversal(),
        jnp.where(counted, 0.0, score[64:128]),
        precision=lax.Precision.HIGHEST,
        preferred_element_type=F32,
    )

    tail_g = jnp.where(y == 0, g, next_g)
    targets = [(g, z, y), (tail_g, z, 3 - y), (g, 15 - z, y)]

    def sc_copy(k, gg, ss, at):
        return pltpu.make_async_remote_copy(
            src_ref=sc_send.at[k],
            dst_ref=sc_recv.at[at],
            send_sem=sc_ssem.at[k],
            recv_sem=sc_rsem.at[at],
            device_id=(gg, ss),
            device_id_type=MESH,
        )

    def own(k):
        if k == 0:
            return s == z
        if k == 1:
            return jnp.logical_and(y == 0, s == z)
        return s == 15 - z

    for k, (gg, ss, at) in enumerate(targets):

        @pl.when(jnp.logical_not(own(k)))
        def _():
            sc_copy(k, gg, ss, at).start()

        @pl.when(own(k))
        def _():
            sc_recv[at] = sc_send[k]

    @pl.when(jnp.logical_not(low))
    def _():
        sc_recv[2] = jnp.zeros((64, 64), F32)
        sc_recv[3] = jnp.zeros((64, 64), F32)

    @pl.when(jnp.logical_and(s != 0, s != 10))
    def _():
        sc_copy(0, g, s, 0).wait_recv()

    sc_copy(0, g, s, 1).wait_recv()

    @pl.when(low)
    def _():
        sc_copy(0, g, s, 2).wait_recv()

        @pl.when(s != 0)
        def _():
            sc_copy(0, g, s, 3).wait_recv()

    row = 64 * s + lax.broadcasted_iota(jnp.int32, (64, 64), 0)
    for a in range(2):
        slot = 2 * g + a
        gone = jnp.where(slot < lens_ref.shape[0], lens_ref[jnp.minimum(slot, lens_ref.shape[0] - 1)], 0)
        step = lat_ref[a] + STEP * (sc_recv[a] + sc_recv[2 + a])
        out_ref[a] = jnp.where(row < 1024 - gone, step, 0.0)

    lat_sends(lambda c: c.wait_send())

    @pl.loop(1, 16)
    def _(k):
        fold_copy(k, s, s).wait_send()
        to_sib((s + k) % 16).wait_send()

    for t in range(4):
        ring_far(t).wait_send()
    for t in range(3):
        ring_near(t).wait_send()

    @pl.loop(0, 8)
    def _(k):
        across(2 * k + y).wait_send()

    for k in range(3):

        @pl.when(jnp.logical_not(own(k)))
        def _():
            sc_copy(k, g, s, 0).wait_send()


def solution(mesh):
    groups = mesh.shape["group"]

    def body(latent, margin_len, in_weight, norm_gain, qkv_weight, out_weight, final_gain, head_out):
        width = in_weight.shape[1]
        vmem = pl.BlockSpec(memory_space=pltpu.VMEM)
        hbm = pl.BlockSpec(memory_space=pl.ANY)
        dma = pltpu.SemaphoreType.DMA
        return pl.pallas_call(
            functools.partial(kernel, groups),
            out_shape=jax.ShapeDtypeStruct(latent.shape, F32),
            in_specs=[
                vmem,
                pl.BlockSpec(memory_space=pltpu.SMEM),
                vmem,
                vmem,
                hbm,
                hbm,
                vmem,
                hbm,
            ],
            out_specs=vmem,
            scratch_shapes=[
                pltpu.VMEM(qkv_weight.shape, BF),
                pltpu.VMEM(out_weight.shape, BF),
                pltpu.VMEM(head_out.shape, BF),
                pltpu.VMEM((2, PACK, 128), BF),
                pltpu.VMEM((24, PACK, 128), BF),
                pltpu.VMEM((1024, 128), BF),
                pltpu.VMEM((2, 1024, width // 2), BF),
                pltpu.VMEM((128, 1024), BF),
                pltpu.VMEM((512, 128), BF),
                pltpu.VMEM((512, 256), BF),
                pltpu.VMEM((192, 1024), BF),
                pltpu.VMEM((3, 64, 64), F32),
                pltpu.VMEM((4, 64, 64), F32),
                dma((3,)),
                dma((4, 8)),
                dma((24,)),
                dma((16,)),
                dma((16,)),
                dma((2, 4)),
                dma((8,)),
                dma((16,)),
                dma((2, 16)),
                dma((3,)),
                dma((4,)),
            ],
            compiler_params=pltpu.CompilerParams(
                collective_id=0, has_side_effects=True, vmem_limit_bytes=48 * 1024 * 1024
            ),
        )(
            latent,
            margin_len,
            in_weight,
            norm_gain.reshape(1, width),
            qkv_weight,
            out_weight,
            final_gain.reshape(1, width),
            head_out,
        )

    in_specs = (
        P("group", "seq", None),
        P(),
        P(),
        P(),
        P(None, None, "seq"),
        P("seq", None),
        P(),
        P(),
    )
    return jax.shard_map(
        body, mesh=mesh, in_specs=in_specs, out_specs=P("group", "seq", None), check_vma=False
    )
```

time: 178 us -> 60.3 us (0.34)
  the two profiles are of different devices: /device:TPU:16 before, /device:TPU:72 now
where the time goes in v1:
time: 60.3 us; the launch traced here: 60.2 us
  Pallas kernels  55.2 us (92%)
  local copies, waits for them, and re-layouts  4.89 us (8%)
    pallas_call x1, Pallas kernels, body(): pl.pallas_call(functools.partial(kernel, groups), out_shape=jax.ShapeDtyp...  55.2 us
    unnamed x11, local copies, waits for them, and re-layouts  3.49 us

profile of v1, /device:TPU:72, one launch (start us, length us, event | category | flops | bytes accessed | tf_op | source)
XLA Modules:
  0.0 60.2 jit_solution(14999099631052121922)
XLA Ops:
  0.0 0.7 %reshape.6.gain_ref = f32[1,1536]{1,0:T(1,128)S(1)} reshape(f32[1536]{0:T(1024)} %param.11) | data formatting | bytes 12288 | tf_op jit(solution)/shard_map/reshape | solution.py:550
  0.7 0.7 %reshape.7.fgain_ref = f32[1,1536]{1,0:T(1,128)S(1)} reshape(f32[1536]{0:T(1024)} %param.14) | data formatting | bytes 12288 | tf_op jit(solution)/shard_map/reshape | solution.py:553
  1.4 0.0 copy-start
  1.4 0.0 copy-start.1
  1.4 0.0 copy-start.2
  1.4 0.0 copy-start.3
  1.4 1.2 %copy.10.ho_hbm = bf16[1536,64]{1,0:T(8,128)(2,1)S(1)} copy(bf16[1536,64]{0,1:T(8,128)(2,1)} %param.15) | data formatting | bytes 393216 | tf_op args[7]
  2.6 1.6 %copy.9.qkv_hbm = bf16[3,1536,64]{2,1,0:T(8,128)(2,1)S(1)} copy(bf16[3,1536,64]{1,2,0:T(8,128)(2,1)} %param.12) | data formatting | bytes 1179648 | tf_op args[4]
  4.3 0.0 copy-done
  4.3 0.0 copy-done.1
  4.3 0.0 copy-done.2
  4.3 0.0 copy-done.3
  4.3 55.2 %shard_map.82 = f32[2,64,64]{2,1,0:T(8,128)S(1)} custom-call(f32[2,64,64]{2,1,0:T(8,128)S(1)} %copy-done.2, s32[31]{0:T(128)S(1)} %copy-done.3, bf16[64,1536]{1,0:T(8,128)(2,1)S(1)} %copy-done, f32[1,1536]{1,0:T(1,128)S(1)} %reshape.6.gain_ref, bf16[3,1536,64]{2,1,0:T(8,128)(2,1)S(1)} %copy.9.qkv_hbm, bf16[64,1536]{1,0:T(8,128)(2,1)S(1)} %copy-done.1, ...), custom_call_target="tpu_custom_call" | custom-call | tf_op jit(solution)/shard_map/pallas_call | solution.py:503
  59.5 0.6 %copy.12 = f32[2,64,64]{2,1,0:T(8,128)} copy(f32[2,64,64]{2,1,0:T(8,128)S(1)} %shard_map.82) | data formatting | bytes 65536
Async XLA Ops:
  1.4 2.9 %copy-start = (bf16[64,1536]{1,0:T(8,128)(2,1)S(1)}, bf16[64,1536]{1,0:T(8,128)(2,1)}, u32[]{:S(2)}) copy-start(bf16[64,1536]{1,0:T(8,128)(2,1)} %wi_ref.1) | copy-start | bytes 589828
  1.4 2.9 %copy-start.1 = (bf16[64,1536]{1,0:T(8,128)(2,1)S(1)}, bf16[64,1536]{1,0:T(8,128)(2,1)}, u32[]{:S(2)}) copy-start(bf16[64,1536]{1,0:T(8,128)(2,1)} %o_hbm.1) | copy-start | bytes 589828
  1.4 2.9 %copy-start.2 = (f32[2,64,64]{2,1,0:T(8,128)S(1)}, f32[2,64,64]{2,1,0:T(8,128)}, u32[]{:S(2)}) copy-start(f32[2,64,64]{2,1,0:T(8,128)} %lat_ref.1) | copy-start | bytes 98308
  1.4 2.9 %copy-start.3 = (s32[31]{0:T(128)S(1)}, s32[31]{0:T(128)}, u32[]{:S(2)}) copy-start(s32[31]{0:T(128)} %lens_ref.1) | copy-start | bytes 376

commit v2 on v1

v2 whole, which is shorter than its diff:
```python
import functools
import math

import jax
import jax.numpy as jnp
from jax import lax
from jax.experimental import pallas as pl
from jax.experimental.pallas import tpu as pltpu
from jax.sharding import PartitionSpec as P

MESH = pl.DeviceIdType.MESH
BF = jnp.bfloat16
F32 = jnp.float32

HDIM = 64
STEP = -0.5
ROWS = 64
PACK = 32
QSCALE = HDIM**-0.5 * math.log2(math.e)


def dot(a, b):
    return jnp.dot(a, b, preferred_element_type=F32)


def dot_nt(a, b):
    return lax.dot_general(a, b, (((1,), (1,)), ((), ())), preferred_element_type=F32)


def hi_lo(x):
    hi = x.astype(BF)
    return hi, (x - hi.astype(F32)).astype(BF)


def packed(x):
    return jnp.concatenate([x[:PACK], x[PACK:]], axis=1)


def unpacked(x):
    return jnp.concatenate([x[:, :HDIM], x[:, HDIM:]], axis=0)


def reversal():
    r = lax.broadcasted_iota(jnp.int32, (ROWS, ROWS), 0)
    c = lax.broadcasted_iota(jnp.int32, (ROWS, ROWS), 1)
    return (r + c == ROWS - 1).astype(F32)


def kernel(
    groups,
    lat_hbm,
    lens_hbm,
    wi_hbm,
    gain_hbm,
    qkv_hbm,
    o_hbm,
    fgain_hbm,
    ho_hbm,
    out_ref,
    lat_ref,
    lens_ref,
    wi_ref,
    gain_ref,
    qkv_v,
    fgain_ref,
    ho_v,
    lat_send,
    lat_ht,
    lat_r,
    fold_buf,
    o_buf,
    xkt,
    w_head,
    w_tail,
    att,
    sc_send,
    sc_recv,
    load_sem,
    own_sem,
    lat_ssem,
    lat_rsem,
    fold_ssem,
    fsib_ssem,
    fold_rsem,
    z_ssem,
    y_ssem,
    x_ssem,
    sib_ssem,
    o_rsem,
    sc_ssem,
    sc_rsem,
):
    g = lax.axis_index("group")
    s = lax.axis_index("seq")
    z = s // 2
    y = s % 2
    core = g % 2
    prev_g = (g + groups - 1) % groups
    next_g = (g + 1) % groups
    sib_g = g + 1 - 2 * core
    y_g = (g + core * (groups // 2)) % groups
    y_s = 2 * z + 1 - y
    x = (g // 2) % 4
    px = x % 2
    x_step = jnp.where(core == 0, 1 - 2 * px, 2 * px - 1)
    x_g = g + 2 * ((x + x_step + 4) % 4 - x)
    mine = 2 * px + core
    low = s < 8
    quarter = o_buf.shape[2]

    def block_rows(block):
        return pl.ds(pl.multiple_of(block * 64, 64), 64)

    load_lat, load_lens, load_wi, load_gain, load_qkv, load_fgain, load_ho = [
        pltpu.make_async_copy(src, dst, load_sem.at[k])
        for k, (src, dst) in enumerate(
            [
                (lat_hbm, lat_ref),
                (lens_hbm, lens_ref),
                (wi_hbm, wi_ref),
                (gain_hbm, gain_ref),
                (qkv_hbm, qkv_v),
                (fgain_hbm, fgain_ref),
                (ho_hbm, ho_v),
            ]
        )
    ]
    load_o = [
        pltpu.make_async_copy(
            o_hbm.at[:, pl.ds(k * quarter, quarter)], o_buf.at[k, block_rows(s)], own_sem.at[k]
        )
        for k in range(4)
    ]
    for load in [load_lat, load_wi, load_gain, load_qkv, *load_o, load_lens, load_fgain, load_ho]:
        load.start()

    barrier = pltpu.get_barrier_semaphore()

    def greet(gg, ss):
        pl.semaphore_signal(barrier, inc=1, device_id=(gg, ss), device_id_type=MESH)

    @pl.loop(1, 16)
    def _(k):
        greet(g, (s + k) % 16)

    @pl.when(low)
    def _():
        @pl.loop(0, 8)
        def _(k):
            greet(prev_g, 2 * k + 1)

    @pl.when(y == 1)
    def _():
        @pl.loop(0, 8)
        def _(k):
            greet(next_g, k)

    greet(sib_g, s)
    greet(x_g, s)

    @pl.when(core == 1)
    def _():
        greet(y_g, y_s)

    flip = reversal().astype(BF)
    load_lat.wait()
    for a in range(2):
        rows = lat_ref[a].astype(BF)
        turned = jnp.where(low, rows.astype(F32), dot(flip, rows))
        lat_send[a] = packed(turned).astype(BF)

    n_greet = 17 + jnp.where(low, 8, 0) + jnp.where(y == 1, 8, 0) + core
    pl.semaphore_wait(barrier, n_greet)

    def lat_copy(src, dst, ssem, rsem, gg, ss):
        return pltpu.make_async_remote_copy(
            src_ref=src,
            dst_ref=dst,
            send_sem=ssem,
            recv_sem=lat_rsem.at[rsem],
            device_id=(gg, ss),
            device_id_type=MESH,
        )

    def lat_sends(act):
        @pl.loop(0, 8)
        def _(j):
            k = (z + j + 4) % 8
            near = j == 4

            @pl.when(low)
            def _():
                @pl.when(jnp.logical_not(jnp.logical_and(near, y == 0)))
                def _():
                    act(lat_copy(lat_send, lat_ht.at[s], lat_ssem.at[0, k], s, g, 2 * k))

                @pl.when(jnp.logical_not(jnp.logical_and(near, y == 1)))
                def _():
                    act(
                        lat_copy(
                            lat_send.at[1], lat_ht.at[s, 0], lat_ssem.at[1, k], s, g, 2 * k + 1
                        )
                    )

                act(
                    lat_copy(
                        lat_send.at[0],
                        lat_ht.at[s, 1],
                        lat_ssem.at[2, k],
                        8 + s,
                        prev_g,
                        2 * k + 1,
                    )
                )

            @pl.when(jnp.logical_not(low))
            def _():
                for a in range(2):

                    @pl.when(jnp.logical_not(jnp.logical_and(near, y == a)))
                    def _():
                        act(
                            lat_copy(
                                lat_send.at[a],
                                lat_r.at[15 - s],
                                lat_ssem.at[a, k],
                                31 - s,
                                g,
                                2 * k + a,
                            )
                        )

    lat_sends(lambda c: c.start())

    @pl.when(jnp.logical_and(low, y == 0))
    def _():
        lat_ht[s] = lat_send[...]

    @pl.when(jnp.logical_and(low, y == 1))
    def _():
        lat_ht[s, 0] = lat_send[1]

    @pl.when(jnp.logical_not(low))
    def _():
        lat_r[15 - s] = lat_send[y]

    def o_copy(part, block, ssem, gg, ss):
        return pltpu.make_async_remote_copy(
            src_ref=o_buf.at[part, block_rows(block)],
            dst_ref=o_buf.at[part, block_rows(block)],
            send_sem=ssem,
            recv_sem=o_rsem.at[part, block],
            device_id=(gg, ss),
            device_id_type=MESH,
        )

    def along(d):
        return o_copy(mine, s, z_ssem.at[d], g, 2 * ((z + d) % 8) + y)

    def across(block):
        return o_copy(mine, block, y_ssem.at[block // 2], y_g, y_s)

    def to_x(block):
        return o_copy(mine, block, x_ssem.at[block], x_g, s)

    def to_sib(part, block):
        return o_copy(part, block, sib_ssem.at[part // 2, block], sib_g, s)

    def arrived(part, block):
        o_copy(part, block, z_ssem.at[0], sib_g, s).wait_recv()

    for load in load_o:
        load.wait()
    for d in (4, 3, 5, 2, 6, 1, 7):
        along(d).start()
    across(s).start()

    load_wi.wait()
    load_gain.wait()
    wi = wi_ref[...].astype(F32)
    centred = wi - jnp.mean(wi, axis=1, keepdims=True)
    wg_hi, wg_lo = hi_lo(centred * gain_ref[...].reshape(1, -1))
    wg = jnp.concatenate([wg_hi, wg_lo], axis=0)
    load_qkv.wait()
    fold2 = dot_nt(qkv_v[...].reshape(192, -1), wg)
    fold = fold2[:, :64] + fold2[:, 64:]
    fold_buf[s, 0:64] = jnp.concatenate([fold[:64], fold[64:128]], axis=1).astype(BF)
    fold_buf[s, 64:96] = packed(fold[128:].T).astype(BF)

    def fold_copy(part, block, ssem, gg, ss):
        rows = pl.ds(pl.multiple_of(part * 48, 16), 48)
        return pltpu.make_async_remote_copy(
            src_ref=fold_buf.at[block, rows],
            dst_ref=fold_buf.at[block, rows],
            send_sem=ssem,
            recv_sem=fold_rsem.at[part, block],
            device_id=(gg, ss),
            device_id_type=MESH,
        )

    def fold_out(k):
        return fold_copy(core, s, fold_ssem.at[k], g, (s + k) % 16)

    def fold_sib(block):
        return fold_copy(core, block, fsib_ssem.at[block], sib_g, s)

    def fold_arrived(part, block):
        fold_copy(part, block, fold_ssem.at[0], sib_g, s).wait_recv()

    @pl.loop(0, 15)
    def _(k):
        fold_out((k + 8) % 16 + (k + 8) // 16).start()

    c_hi, c_lo = hi_lo(centred)
    cc = jnp.concatenate([c_hi, c_lo], axis=0)
    gram4 = dot_nt(cc, cc)
    gram2 = gram4[:64] + gram4[64:]
    gram = (gram2[:, :64] + gram2[:, 64:]) * (1.0 / wi.shape[1])
    gram_hi, gram_lo = hi_lo(gram)
    gram_st = jnp.concatenate([gram_hi, gram_lo], axis=0)

    def variance(xt):
        gx = dot(gram_st, xt.astype(BF))
        return jnp.maximum(jnp.sum((gx[:64] + gx[64:]) * xt, axis=0, keepdims=True), 0.0)

    load_lens.wait()
    node = 2 * g + y
    tail_len = jnp.where(node < lens_ref.shape[0], lens_ref[jnp.minimum(node, lens_ref.shape[0] - 1)], 0)

    def lat_arrived(dst, rsem):
        lat_copy(dst, dst, lat_ssem.at[0, 0], rsem, sib_g, s).wait_recv()

    @pl.loop(0, 8)
    def _(k):
        @pl.when(jnp.logical_and(y == 0, k != s))
        def _():
            lat_arrived(lat_ht.at[k], k)

        @pl.when(y == 1)
        def _():
            @pl.when(k != s)
            def _():
                lat_arrived(lat_ht.at[k, 0], k)

            lat_arrived(lat_ht.at[k, 1], 8 + k)

        @pl.when(15 - k != s)
        def _():
            lat_arrived(lat_r.at[k], 16 + k)

    line = lax.broadcasted_iota(jnp.int32, (256, 128), 0)
    lane = lax.broadcasted_iota(jnp.int32, (256, 128), 1)
    spot = 64 * (line // 32) + line % 32 + 32 * (lane // 64)
    head_lines = lat_ht[:, 0].astype(F32).reshape(256, 128)
    tail_lines = jnp.where(
        spot < tail_len,
        lat_ht[:, 1].astype(F32).reshape(256, 128),
        lat_r[...].astype(F32).reshape(256, 128),
    )
    tokens = jnp.concatenate([unpacked(head_lines), unpacked(tail_lines)], axis=0)
    xt = tokens.T
    xkt[0:64, :] = jnp.zeros((64, 1024), BF)
    xkt[64:128, :] = xt.astype(BF)
    var = variance(xt)
    key_eps = 1e-6 * (var + 1e-5)
    scaled = xt * lax.rsqrt(var + 1e-5)
    extra = (lax.broadcasted_iota(jnp.int32, (64, 1024), 0) == 0).astype(F32)
    w = jnp.concatenate([scaled, extra], axis=0).T
    w_head[...] = w[:512].astype(BF)
    place = lax.broadcasted_iota(jnp.int32, (512, 128), 0)
    tail_spot = 64 * ((place % 256) // 32) + place % 32 + 32 * (place // 256)
    w_tail[:, :128] = w[512:].astype(BF)
    w_tail[:, 128:] = jnp.where(tail_spot < tail_len, w[512:], 0.0).astype(BF)

    q_line = lax.broadcasted_iota(jnp.int32, (32, 128), 0)
    q_lane = lax.broadcasted_iota(jnp.int32, (32, 128), 1)
    q_spot = 64 * z + q_line + 32 * (q_lane // 64)
    q_tail = jnp.where(q_spot < tail_len, lat_ht[z, 1].astype(F32), lat_r[z].astype(F32))
    q_tok = jnp.concatenate([unpacked(lat_ht[z, 0].astype(F32)), unpacked(q_tail)], axis=0)
    q_xt = q_tok.T
    q_eps = 1e-6 * (variance(q_xt) + 1e-5)
    q_xtz = jnp.concatenate([q_xt.astype(BF), jnp.zeros((64, 128), BF)], axis=0)
    q_side = lax.broadcasted_iota(jnp.int32, (128, 128), 1) < 64

    def rms(x, eps, scale):
        parts = []
        for h in range(2):
            rows = x[64 * h : 64 * h + 64]
            mean = jnp.sum(rows * rows, axis=0, keepdims=True) * (1.0 / HDIM)
            parts.append(rows * (lax.rsqrt(mean + eps) * scale))
        return jnp.concatenate(parts, axis=0)

    def place(n):
        return (z + jnp.where(n % 2 == 1, (n + 1) // 2, 8 - n // 2)) % 8

    def fold_relay(n):
        for h in range(2):
            block = 2 * place(n) + h

            @pl.when(block != s)
            def _():
                fold_arrived(core, block)
                fold_sib(block).start()

    def out_of(d):
        return [2 * ((z + d) % 8) + y, 2 * ((z + 8 - d) % 8) + y]

    def pass_on_z(d):
        for k, block in enumerate(out_of(d)):

            @pl.when(jnp.logical_or(d != 4, k == 0))
            def _():
                arrived(mine, block)
                across(block).start()
                to_x(block).start()
                to_sib(mine, block).start()

    def pass_on_y(d):
        for k, block in enumerate(out_of(d)):

            @pl.when(jnp.logical_or(jnp.logical_and(d != 4, d != 0), k == 0))
            def _():
                other = block + 1 - 2 * y
                arrived(mine, other)
                to_x(other).start()
                to_sib(mine, other).start()

    theirs = 2 * (1 - px) + core

    def pass_on_x(d, side):
        for k, block in enumerate(out_of(d)):

            @pl.when(jnp.logical_or(jnp.logical_and(d != 4, d != 0), k == 0))
            def _():
                there = block + (1 - 2 * y) * side
                arrived(theirs, there)
                to_sib(theirs, there).start()

    fold_relay(0)

    @pl.loop(0, 8)
    def _(n):
        @pl.when(n < 7)
        def _():
            fold_relay(n + 1)

        zz = place(n)
        for h in range(2):

            @pl.when(2 * zz + h != s)
            def _():
                fold_arrived(1 - core, 2 * zz + h)

        pair = fold_buf[pl.ds(2 * zz, 2)]
        pair_qk = jnp.concatenate([pair[0, :64], pair[1, :64]], axis=0)
        keys_t = rms(dot(pair_qk, xkt[...]), key_eps, 1.0).astype(BF)
        query = rms(dot(pair_qk, q_xtz), q_eps, QSCALE).T
        query2 = jnp.concatenate(
            [jnp.where(q_side, query, 0.0), jnp.where(q_side, 0.0, query)], axis=0
        ).astype(BF)
        p = jnp.exp2(dot(query2, keys_t)).astype(BF)
        u_head = dot(p[:, :512], w_head[...])
        u_tail = dot(p[:, 512:], w_tail[...])
        u_all = u_head + u_tail[:, :128]
        ratio = u_all[:, :64] / u_all[:, 64:65]
        u_over = jnp.concatenate([u_tail[64:128, 128:], u_tail[192:256, 128:]], axis=0)
        total = u_over[:, 64:65]
        over = u_over[:, :64] / jnp.where(total == 0.0, 1.0, total)
        mean_even = jnp.concatenate([ratio[:128], over[:64]], axis=0).astype(BF)
        mean_odd = jnp.concatenate([ratio[128:], over[64:]], axis=0).astype(BF)
        att_even = dot(mean_even, unpacked(pair[0, 64:96].astype(F32)).astype(BF))
        att_odd = dot(mean_odd, unpacked(pair[1, 64:96].astype(F32)).astype(BF))
        columns = pl.ds(pl.multiple_of(zz * 128, 128), 128)
        att[:, columns] = jnp.concatenate([att_even, att_odd], axis=1).astype(BF)

        @pl.when(n < 4)
        def _():
            pass_on_z(n + 1)

        @pl.when(jnp.logical_and(n >= 2, n < 7))
        def _():
            pass_on_y(n - 2)

        @pl.when(n >= 4)
        def _():
            pass_on_x(n - 3, 0)

    @pl.loop(0, 5)
    def _(d):
        pass_on_x(d, 1)

    @pl.loop(1, 16)
    def _(k):
        for half in range(2):
            arrived(2 * half + 1 - core, (s + k) % 16)

    tok2 = jnp.concatenate([q_tok, q_tok[64:]], axis=0).astype(BF)
    mixed = jnp.concatenate(
        [
            dot(att[...], o_buf[k]) + dot(tok2, wi_ref[:, k * quarter : (k + 1) * quarter])
            for k in range(4)
        ],
        axis=1,
    )
    mean = jnp.mean(mixed, axis=1, keepdims=True)
    centre = mixed - mean
    spread = jnp.mean(centre * centre, axis=1, keepdims=True)
    load_fgain.wait()
    load_ho.wait()
    final = (centre * lax.rsqrt(spread + 1e-5) * fgain_ref[...].reshape(1, -1)).astype(BF)
    score = dot_nt(final, ho_v[...])

    where_t = 64 * z + lax.broadcasted_iota(jnp.int32, (64, 64), 0)
    counted = where_t < tail_len
    sc_send[0] = score[:64]
    sc_send[1] = jnp.where(counted, score[64:128] - score[128:], 0.0)
    sc_send[2] = jnp.dot(
        reversal(),
        jnp.where(counted, 0.0, score[64:128]),
        precision=lax.Precision.HIGHEST,
        preferred_element_type=F32,
    )

    tail_g = jnp.where(y == 0, g, next_g)
    targets = [(g, z, y), (tail_g, z, 3 - y), (g, 15 - z, y)]

    def sc_copy(k, gg, ss, at):
        return pltpu.make_async_remote_copy(
            src_ref=sc_send.at[k],
            dst_ref=sc_recv.at[at],
            send_sem=sc_ssem.at[k],
            recv_sem=sc_rsem.at[at],
            device_id=(gg, ss),
            device_id_type=MESH,
        )

    def own(k):
        if k == 0:
            return s == z
        if k == 1:
            return jnp.logical_and(y == 0, s == z)
        return s == 15 - z

    for k, (gg, ss, at) in enumerate(targets):

        @pl.when(jnp.logical_not(own(k)))
        def _():
            sc_copy(k, gg, ss, at).start()

        @pl.when(own(k))
        def _():
            sc_recv[at] = sc_send[k]

    @pl.when(jnp.logical_not(low))
    def _():
        sc_recv[2] = jnp.zeros((64, 64), F32)
        sc_recv[3] = jnp.zeros((64, 64), F32)

    @pl.when(jnp.logical_and(s != 0, s != 10))
    def _():
        sc_copy(0, g, s, 0).wait_recv()

    sc_copy(0, g, s, 1).wait_recv()

    @pl.when(low)
    def _():
        sc_copy(0, g, s, 2).wait_recv()

        @pl.when(s != 0)
        def _():
            sc_copy(0, g, s, 3).wait_recv()

    row = 64 * s + lax.broadcasted_iota(jnp.int32, (64, 64), 0)
    for a in range(2):
        slot = 2 * g + a
        gone = jnp.where(slot < lens_ref.shape[0], lens_ref[jnp.minimum(slot, lens_ref.shape[0] - 1)], 0)
        step = lat_ref[a] + STEP * (sc_recv[a] + sc_recv[2 + a])
        out_ref[a] = jnp.where(row < 1024 - gone, step, 0.0)

    lat_sends(lambda c: c.wait_send())

    @pl.loop(1, 16)
    def _(k):
        there = (s + k) % 16
        fold_out(k).wait_send()
        fold_sib(there).wait_send()
        to_x(there).wait_send()
        to_sib(mine, there).wait_send()
        to_sib(theirs, there).wait_send()

    @pl.loop(1, 8)
    def _(d):
        along(d).wait_send()

    @pl.loop(0, 8)
    def _(k):
        across(2 * k + y).wait_send()

    for k in range(3):

        @pl.when(jnp.logical_not(own(k)))
        def _():
            sc_copy(k, g, s, 0).wait_send()


def solution(mesh):
    groups = mesh.shape["group"]

    def body(latent, margin_len, in_weight, norm_gain, qkv_weight, out_weight, final_gain, head_out):
        width = in_weight.shape[1]
        vmem = pl.BlockSpec(memory_space=pltpu.VMEM)
        hbm = pl.BlockSpec(memory_space=pl.ANY)
        dma = pltpu.SemaphoreType.DMA
        return pl.pallas_call(
            functools.partial(kernel, groups),
            out_shape=jax.ShapeDtypeStruct(latent.shape, F32),
            in_specs=[hbm] * 8,
            out_specs=vmem,
            scratch_shapes=[
                pltpu.VMEM(latent.shape, F32),
                pltpu.SMEM(margin_len.shape, jnp.int32),
                pltpu.VMEM(in_weight.shape, BF),
                pltpu.VMEM((width,), F32),
                pltpu.VMEM((3, HDIM, width), BF),
                pltpu.VMEM((width,), F32),
                pltpu.VMEM(head_out.shape[::-1], BF),
                pltpu.VMEM((2, PACK, 128), BF),
                pltpu.VMEM((8, 2, PACK, 128), BF),
                pltpu.VMEM((8, PACK, 128), BF),
                pltpu.VMEM((16, 96, 128), BF),
                pltpu.VMEM((4, 1024, width // 4), BF),
                pltpu.VMEM((128, 1024), BF),
                pltpu.VMEM((512, 128), BF),
                pltpu.VMEM((512, 256), BF),
                pltpu.VMEM((192, 1024), BF),
                pltpu.VMEM((3, 64, 64), F32),
                pltpu.VMEM((4, 64, 64), F32),
                dma((7,)),
                dma((4,)),
                dma((3, 8)),
                dma((24,)),
                dma((16,)),
                dma((16,)),
                dma((2, 16)),
                dma((8,)),
                dma((8,)),
                dma((16,)),
                dma((2, 16)),
                dma((4, 16)),
                dma((3,)),
                dma((4,)),
            ],
            compiler_params=pltpu.CompilerParams(
                collective_id=0, has_side_effects=True, vmem_limit_bytes=60 * 1024 * 1024
            ),
        )(
            latent,
            margin_len,
            in_weight,
            norm_gain,
            jnp.swapaxes(qkv_weight, 1, 2),
            out_weight,
            final_gain,
            head_out.T,
        )

    in_specs = (
        P("group", "seq", None),
        P(),
        P(),
        P(),
        P(None, None, "seq"),
        P("seq", None),
        P(),
        P(),
    )
    return jax.shard_map(
        body, mesh=mesh, in_specs=in_specs, out_specs=P("group", "seq", None), check_vma=False
    )
```

time: 60.3 us -> 55.7 us (0.924)
  the two profiles are of different devices: /device:TPU:72 before, /device:TPU:8 now
where the time goes in v2:
time: 55.7 us; the launch traced here: 55.1 us
  Pallas kernels  53.7 us (96%)
  local copies, waits for them, and re-layouts  1.47 us (3%)
    pallas_call x1, Pallas kernels, body(): pl.pallas_call(functools.partial(kernel, groups), out_shape=jax.ShapeDtyp...  53.7 us
    unnamed x1, local copies, waits for them, and re-layouts  1.47 us

profile of v2, /device:TPU:8, one launch (start us, length us, event | category | flops | bytes accessed | tf_op | source)
XLA Modules:
  0.0 55.1 jit_solution(10529012882023949440)
XLA Ops:
  0.0 53.7 %shard_map.82 = f32[2,64,64]{2,1,0:T(8,128)} custom-call(f32[2,64,64]{2,1,0:T(8,128)} %lat_hbm.1, s32[31]{0:T(128)} %lens_hbm.1, bf16[64,1536]{1,0:T(8,128)(2,1)} %wi_hbm.1, f32[1536]{0:T(1024)} %gain_hbm.1, bf16[3,64,1536]{2,1,0:T(8,128)(2,1)} %bitcast.2, bf16[64,1536]{1,0:T(8,128)(2,1)} %o_hbm.1, f32[1536]{0:T(1024)} %fgain_hbm.1, bf16[64,1536]{1,0:T(8,128)(2,1)} %bitcast.3), custom_call_target="tpu_custom_call" | custom-call | tf_op jit(solution)/shard_map/pallas_call | solution.py:614
  53.7 1.5 %copy.10 = f32[2,64,64]{2,1,0:T(8,128)} copy(f32[2,64,64]{2,1,0:T(8,128)} %shard_map.82) | data formatting | bytes 65536

commit v3 on v2

--- a/solution.py
+++ b/solution.py
@@ -80,6 +80,7 @@
     lat_ssem,
     lat_rsem,
     fold_ssem,
+    fy_ssem,
     fsib_ssem,
     fold_rsem,
     z_ssem,
@@ -105,7 +106,10 @@
     x_step = jnp.where(core == 0, 1 - 2 * px, 2 * px - 1)
     x_g = g + 2 * ((x + x_step + 4) % 4 - x)
     mine = 2 * px + core
+    me = 8 * y + z
     low = s < 8
+    head_block = (z + 2) % 8
+    tail_block = jnp.where(z < 4, 4 * (z // 2) + 2 * (1 - z % 2), (2 * z + 5) % 8)
     quarter = o_buf.shape[2]
 
     def block_rows(block):
@@ -127,7 +131,7 @@
     ]
     load_o = [
         pltpu.make_async_copy(
-            o_hbm.at[:, pl.ds(k * quarter, quarter)], o_buf.at[k, block_rows(s)], own_sem.at[k]
+            o_hbm.at[:, pl.ds(k * quarter, quarter)], o_buf.at[k, block_rows(me)], own_sem.at[k]
         )
         for k in range(4)
     ]
@@ -254,11 +258,26 @@
             device_id_type=MESH,
         )
 
-    def along(d):
-        return o_copy(mine, s, z_ssem.at[d], g, 2 * ((z + d) % 8) + y)
+    def seq_at(d):
+        return 2 * ((z + d + 8) % 8) + y
+
+    def column(d):
+        return 8 * y + (z + d + 8) % 8
+
+    def other(d):
+        return 8 * (1 - y) + (z + d + 8) % 8
+
+    def along(k, d):
+        return o_copy(mine, me, z_ssem.at[k], g, seq_at(d))
+
+    firsts = [along(k, d) for k, d in enumerate((2, -2, 1, -1))]
+    side = 1 - 2 * core
+    on_up = o_copy(mine, column(-2), z_ssem.at[4], g, seq_at(1))
+    on_down = o_copy(mine, column(2), z_ssem.at[5], g, seq_at(-1))
+    on_far = o_copy(mine, column(-2 * side), z_ssem.at[6], g, seq_at(2 * side))
 
     def across(block):
-        return o_copy(mine, block, y_ssem.at[block // 2], y_g, y_s)
+        return o_copy(mine, block, y_ssem.at[block % 8], y_g, y_s)
 
     def to_x(block):
         return o_copy(mine, block, x_ssem.at[block], x_g, s)
@@ -268,12 +287,6 @@
 
     def arrived(part, block):
         o_copy(part, block, z_ssem.at[0], sib_g, s).wait_recv()
-
-    for load in load_o:
-        load.wait()
-    for d in (4, 3, 5, 2, 6, 1, 7):
-        along(d).start()
-    across(s).start()
 
     load_wi.wait()
     load_gain.wait()
@@ -284,8 +297,8 @@
     load_qkv.wait()
     fold2 = dot_nt(qkv_v[...].reshape(192, -1), wg)
     fold = fold2[:, :64] + fold2[:, 64:]
-    fold_buf[s, 0:64] = jnp.concatenate([fold[:64], fold[64:128]], axis=1).astype(BF)
-    fold_buf[s, 64:96] = packed(fold[128:].T).astype(BF)
+    fold_buf[me, 0:64] = jnp.concatenate([fold[:64], fold[64:128]], axis=1).astype(BF)
+    fold_buf[me, 64:96] = packed(fold[128:].T).astype(BF)
 
     def fold_copy(part, block, ssem, gg, ss):
         rows = pl.ds(pl.multiple_of(part * 48, 16), 48)
@@ -298,8 +311,11 @@
             device_id_type=MESH,
         )
 
-    def fold_out(k):
-        return fold_copy(core, s, fold_ssem.at[k], g, (s + k) % 16)
+    def fold_out(d):
+        return fold_copy(core, me, fold_ssem.at[d], g, seq_at(d))
+
+    def fold_across(block):
+        return fold_copy(core, block, fy_ssem.at[block % 8], y_g, y_s)
 
     def fold_sib(block):
         return fold_copy(core, block, fsib_ssem.at[block], sib_g, s)
@@ -307,9 +323,15 @@
     def fold_arrived(part, block):
         fold_copy(part, block, fold_ssem.at[0], sib_g, s).wait_recv()
 
-    @pl.loop(0, 15)
-    def _(k):
-        fold_out((k + 8) % 16 + (k + 8) // 16).start()
+    fold_across(me).start()
+    for d in (4, 3, 5, 2, 6, 1, 7):
+        fold_out(d).start()
+
+    for load in load_o:
+        load.wait()
+    for first in firsts:
+        first.start()
+    across(me).start()
 
     c_hi, c_lo = hi_lo(centred)
     cc = jnp.concatenate([c_hi, c_lo], axis=0)
@@ -374,9 +396,9 @@
 
     q_line = lax.broadcasted_iota(jnp.int32, (32, 128), 0)
     q_lane = lax.broadcasted_iota(jnp.int32, (32, 128), 1)
-    q_spot = 64 * z + q_line + 32 * (q_lane // 64)
-    q_tail = jnp.where(q_spot < tail_len, lat_ht[z, 1].astype(F32), lat_r[z].astype(F32))
-    q_tok = jnp.concatenate([unpacked(lat_ht[z, 0].astype(F32)), unpacked(q_tail)], axis=0)
+    q_spot = 64 * tail_block + q_line + 32 * (q_lane // 64)
+    q_tail = jnp.where(q_spot < tail_len, lat_ht[tail_block, 1].astype(F32), lat_r[tail_block].astype(F32))
+    q_tok = jnp.concatenate([unpacked(lat_ht[head_block, 0].astype(F32)), unpacked(q_tail)], axis=0)
     q_xt = q_tok.T
     q_eps = 1e-6 * (variance(q_xt) + 1e-5)
     q_xtz = jnp.concatenate([q_xt.astype(BF), jnp.zeros((64, 128), BF)], axis=0)
@@ -390,68 +412,85 @@
             parts.append(rows * (lax.rsqrt(mean + eps) * scale))
         return jnp.concatenate(parts, axis=0)
 
-    def place(n):
-        return (z + jnp.where(n % 2 == 1, (n + 1) // 2, 8 - n // 2)) % 8
+    def at_step(n):
+        turn = n % 4
+        near = (z // 2 + jnp.where(turn < 2, turn, 5 - turn)) % 4
+        return 8 * jnp.where(n < 4, y, 1 - y) + 2 * near
 
     def fold_relay(n):
         for h in range(2):
-            block = 2 * place(n) + h
-
-            @pl.when(block != s)
+            block = at_step(n) + h
+
+            @pl.when(block != me)
             def _():
                 fold_arrived(core, block)
+
+                @pl.when(n < 4)
+                def _():
+                    fold_across(block).start()
+
                 fold_sib(block).start()
 
-    def out_of(d):
-        return [2 * ((z + d) % 8) + y, 2 * ((z + 8 - d) % 8) + y]
-
-    def pass_on_z(d):
-        for k, block in enumerate(out_of(d)):
-
-            @pl.when(jnp.logical_or(d != 4, k == 0))
+    def around(d, of):
+        return [
+            (of(d), d >= 0),
+            (of(-d), jnp.logical_and(d != 0, d != 4)),
+        ]
+
+    def pass_on_z(i):
+        d = jnp.where(i == 0, 2, jnp.where(i == 1, 1, i + 1))
+        for block, there in around(d, column):
+
+            @pl.when(there)
             def _():
                 arrived(mine, block)
                 across(block).start()
                 to_x(block).start()
                 to_sib(mine, block).start()
 
-    def pass_on_y(d):
-        for k, block in enumerate(out_of(d)):
-
-            @pl.when(jnp.logical_or(jnp.logical_and(d != 4, d != 0), k == 0))
+        @pl.when(i == 0)
+        def _():
+            on_up.start()
+            on_down.start()
+            on_far.start()
+
+    def pass_on_y(i):
+        d = jnp.where(i == 1, 2, jnp.where(i == 2, 1, i))
+        for block, there in around(d, other):
+
+            @pl.when(there)
             def _():
-                other = block + 1 - 2 * y
-                arrived(mine, other)
-                to_x(other).start()
-                to_sib(mine, other).start()
+                arrived(mine, block)
+                to_x(block).start()
+                to_sib(mine, block).start()
 
     theirs = 2 * (1 - px) + core
 
-    def pass_on_x(d, side):
-        for k, block in enumerate(out_of(d)):
-
-            @pl.when(jnp.logical_or(jnp.logical_and(d != 4, d != 0), k == 0))
+    def pass_on_x(d, of):
+        for block, there in around(d, of):
+
+            @pl.when(there)
             def _():
-                there = block + (1 - 2 * y) * side
-                arrived(theirs, there)
-                to_sib(theirs, there).start()
+                arrived(theirs, block)
+                to_sib(theirs, block).start()
 
     fold_relay(0)
+    fold_relay(1)
 
     @pl.loop(0, 8)
     def _(n):
-        @pl.when(n < 7)
-        def _():
-            fold_relay(n + 1)
-
-        zz = place(n)
+        @pl.when(n < 6)
+        def _():
+            fold_relay(n + 2)
+
+        first = at_step(n)
         for h in range(2):
 
-            @pl.when(2 * zz + h != s)
+            @pl.when(first + h != me)
             def _():
-                fold_arrived(1 - core, 2 * zz + h)
-
-        pair = fold_buf[pl.ds(2 * zz, 2)]
+                fold_arrived(1 - core, first + h)
+
+        pair = fold_buf[pl.ds(first, 2)]
         pair_qk = jnp.concatenate([pair[0, :64], pair[1, :64]], axis=0)
         keys_t = rms(dot(pair_qk, xkt[...]), key_eps, 1.0).astype(BF)
         query = rms(dot(pair_qk, q_xtz), q_eps, QSCALE).T
@@ -470,29 +509,29 @@
         mean_odd = jnp.concatenate([ratio[128:], over[64:]], axis=0).astype(BF)
         att_even = dot(mean_even, unpacked(pair[0, 64:96].astype(F32)).astype(BF))
         att_odd = dot(mean_odd, unpacked(pair[1, 64:96].astype(F32)).astype(BF))
-        columns = pl.ds(pl.multiple_of(zz * 128, 128), 128)
+        columns = pl.ds(pl.multiple_of(first * 64, 128), 128)
         att[:, columns] = jnp.concatenate([att_even, att_odd], axis=1).astype(BF)
 
         @pl.when(n < 4)
         def _():
-            pass_on_z(n + 1)
-
-        @pl.when(jnp.logical_and(n >= 2, n < 7))
-        def _():
-            pass_on_y(n - 2)
-
-        @pl.when(n >= 4)
-        def _():
-            pass_on_x(n - 3, 0)
-
-    @pl.loop(0, 5)
-    def _(d):
-        pass_on_x(d, 1)
+            pass_on_z(n)
+
+        @pl.when(jnp.logical_and(n >= 1, n < 6))
+        def _():
+            pass_on_y(n - 1)
+
+        @pl.when(jnp.logical_and(n >= 3, n < 7))
+        def _():
+            i = n - 3
+            pass_on_x(jnp.where(i == 0, 2, jnp.where(i == 1, 1, i + 1)), column)
+
+    for d in (0, 2, 1, 3, 4):
+        pass_on_x(jnp.int32(d), other)
 
     @pl.loop(1, 16)
     def _(k):
         for half in range(2):
-            arrived(2 * half + 1 - core, (s + k) % 16)
+            arrived(2 * half + 1 - core, (me + k) % 16)
 
     tok2 = jnp.concatenate([q_tok, q_tok[64:]], axis=0).astype(BF)
     mixed = jnp.concatenate(
@@ -510,19 +549,20 @@
     final = (centre * lax.rsqrt(spread + 1e-5) * fgain_ref[...].reshape(1, -1)).astype(BF)
     score = dot_nt(final, ho_v[...])
 
-    where_t = 64 * z + lax.broadcasted_iota(jnp.int32, (64, 64), 0)
+    where_t = 64 * tail_block + lax.broadcasted_iota(jnp.int32, (64, 64), 0)
     counted = where_t < tail_len
-    sc_send[0] = score[:64]
-    sc_send[1] = jnp.where(counted, score[64:128] - score[128:], 0.0)
-    sc_send[2] = jnp.dot(
+    sc_send[0] = packed(score[:64])
+    sc_send[1] = packed(jnp.where(counted, score[64:128] - score[128:], 0.0))
+    turned = jnp.dot(
         reversal(),
         jnp.where(counted, 0.0, score[64:128]),
         precision=lax.Precision.HIGHEST,
         preferred_element_type=F32,
     )
+    sc_send[2] = packed(turned)
 
     tail_g = jnp.where(y == 0, g, next_g)
-    targets = [(g, z, y), (tail_g, z, 3 - y), (g, 15 - z, y)]
+    targets = [(g, head_block, y), (tail_g, tail_block, 3 - y), (g, 15 - tail_block, y)]
 
     def sc_copy(k, gg, ss, at):
         return pltpu.make_async_remote_copy(
@@ -534,39 +574,35 @@
             device_id_type=MESH,
         )
 
-    def own(k):
-        if k == 0:
-            return s == z
-        if k == 1:
-            return jnp.logical_and(y == 0, s == z)
-        return s == 15 - z
+    own = [s == head_block, jnp.logical_and(y == 0, s == tail_block), s == 15 - tail_block]
 
     for k, (gg, ss, at) in enumerate(targets):
 
-        @pl.when(jnp.logical_not(own(k)))
+        @pl.when(jnp.logical_not(own[k]))
         def _():
             sc_copy(k, gg, ss, at).start()
 
-        @pl.when(own(k))
+        @pl.when(own[k])
         def _():
             sc_recv[at] = sc_send[k]
 
     @pl.when(jnp.logical_not(low))
     def _():
-        sc_recv[2] = jnp.zeros((64, 64), F32)
-        sc_recv[3] = jnp.zeros((64, 64), F32)
-
-    @pl.when(jnp.logical_and(s != 0, s != 10))
-    def _():
-        sc_copy(0, g, s, 0).wait_recv()
-
-    sc_copy(0, g, s, 1).wait_recv()
+        sc_recv[2] = jnp.zeros((PACK, 128), F32)
+        sc_recv[3] = jnp.zeros((PACK, 128), F32)
+
+    kept = jnp.logical_or(own[0], own[2])
+    for a in range(2):
+
+        @pl.when(jnp.logical_not(jnp.logical_and(kept, y == a)))
+        def _():
+            sc_copy(0, g, s, a).wait_recv()
 
     @pl.when(low)
     def _():
         sc_copy(0, g, s, 2).wait_recv()
 
-        @pl.when(s != 0)
+        @pl.when(jnp.logical_not(own[1]))
         def _():
             sc_copy(0, g, s, 3).wait_recv()
 
@@ -574,15 +610,14 @@
     for a in range(2):
         slot = 2 * g + a
         gone = jnp.where(slot < lens_ref.shape[0], lens_ref[jnp.minimum(slot, lens_ref.shape[0] - 1)], 0)
-        step = lat_ref[a] + STEP * (sc_recv[a] + sc_recv[2 + a])
+        step = lat_ref[a] + STEP * unpacked(sc_recv[a] + sc_recv[2 + a])
         out_ref[a] = jnp.where(row < 1024 - gone, step, 0.0)
 
     lat_sends(lambda c: c.wait_send())
 
     @pl.loop(1, 16)
     def _(k):
-        there = (s + k) % 16
-        fold_out(k).wait_send()
+        there = (me + k) % 16
         fold_sib(there).wait_send()
         to_x(there).wait_send()
         to_sib(mine, there).wait_send()
@@ -590,15 +625,19 @@
 
     @pl.loop(1, 8)
     def _(d):
-        along(d).wait_send()
+        fold_out(d).wait_send()
+
+    for sent in (*firsts, on_up, on_down, on_far):
+        sent.wait_send()
 
     @pl.loop(0, 8)
     def _(k):
-        across(2 * k + y).wait_send()
+        across(8 * y + k).wait_send()
+        fold_across(8 * y + k).wait_send()
 
     for k in range(3):
 
-        @pl.when(jnp.logical_not(own(k)))
+        @pl.when(jnp.logical_not(own[k]))
         def _():
             sc_copy(k, g, s, 0).wait_send()
 
@@ -633,13 +672,14 @@
                 pltpu.VMEM((512, 128), BF),
                 pltpu.VMEM((512, 256), BF),
                 pltpu.VMEM((192, 1024), BF),
-                pltpu.VMEM((3, 64, 64), F32),
-                pltpu.VMEM((4, 64, 64), F32),
+                pltpu.VMEM((3, PACK, 128), F32),
+                pltpu.VMEM((4, PACK, 128), F32),
                 dma((7,)),
                 dma((4,)),
                 dma((3, 8)),
                 dma((24,)),
-                dma((16,)),
+                dma((8,)),
+                dma((8,)),
                 dma((16,)),
                 dma((2, 16)),
                 dma((8,)),

time: 55.7 us -> 48.9 us (0.88)
  Pallas kernels: 53.7 us -> 47.3 us
    pallas_call x1, Pallas kernels: 53.7 us -> 47.3 us  [body(): pl.pallas_call(functools.partial(kernel, groups), out_shape=jax.ShapeDtyp...]
where the time goes in v3:
time: 48.9 us; the launch traced here: 48.8 us
  Pallas kernels  47.3 us (97%)
  local copies, waits for them, and re-layouts  1.47 us (3%)
    pallas_call x1, Pallas kernels, body(): pl.pallas_call(functools.partial(kernel, groups), out_shape=jax.ShapeDtyp...  47.3 us
    unnamed x1, local copies, waits for them, and re-layouts  1.47 us

profile of v3, /device:TPU:8, one launch (start us, length us, event | category | flops | bytes accessed | tf_op | source)
XLA Modules:
  0.0 48.8 jit_solution(18341338796649086432)
XLA Ops:
  0.0 47.3 %shard_map.82 = f32[2,64,64]{2,1,0:T(8,128)} custom-call(f32[2,64,64]{2,1,0:T(8,128)} %lat_hbm.1, s32[31]{0:T(128)} %lens_hbm.1, bf16[64,1536]{1,0:T(8,128)(2,1)} %wi_hbm.1, f32[1536]{0:T(1024)} %gain_hbm.1, bf16[3,64,1536]{2,1,0:T(8,128)(2,1)} %bitcast.2, bf16[64,1536]{1,0:T(8,128)(2,1)} %o_hbm.1, f32[1536]{0:T(1024)} %fgain_hbm.1, bf16[64,1536]{1,0:T(8,128)(2,1)} %bitcast.3), custom_call_target="tpu_custom_call" | custom-call | tf_op jit(solution)/shard_map/pallas_call | solution.py:653
  47.3 1.5 %copy.10 = f32[2,64,64]{2,1,0:T(8,128)} copy(f32[2,64,64]{2,1,0:T(8,128)} %shard_map.82) | data formatting | bytes 65536

commit v4 on v3

--- a/solution.py
+++ b/solution.py
@@ -65,14 +65,16 @@
     fgain_ref,
     ho_v,
     lat_send,
-    lat_ht,
-    lat_r,
+    lat_tok,
+    lat_next,
     fold_buf,
+    gram_buf,
     o_buf,
     xkt,
     w_head,
     w_tail,
     att,
+    mix,
     sc_send,
     sc_recv,
     load_sem,
@@ -135,9 +137,6 @@
         )
         for k in range(4)
     ]
-    for load in [load_lat, load_wi, load_gain, load_qkv, *load_o, load_lens, load_fgain, load_ho]:
-        load.start()
-
     barrier = pltpu.get_barrier_semaphore()
 
     def greet(gg, ss):
@@ -147,17 +146,18 @@
     def _(k):
         greet(g, (s + k) % 16)
 
+    asker = jnp.where(
+        s % 2 == 0, 2 * ((s % 8) // 4) + 1 - (s // 2) % 2, 4 + ((s + 3) % 8) // 2
+    )
+    greet(jnp.where(low, prev_g, next_g), 15 - s)
+
     @pl.when(low)
     def _():
-        @pl.loop(0, 8)
-        def _(k):
-            greet(prev_g, 2 * k + 1)
+        greet(prev_g, 2 * asker + 1)
 
     @pl.when(y == 1)
     def _():
-        @pl.loop(0, 8)
-        def _(k):
-            greet(next_g, k)
+        greet(next_g, tail_block)
 
     greet(sib_g, s)
     greet(x_g, s)
@@ -165,6 +165,9 @@
     @pl.when(core == 1)
     def _():
         greet(y_g, y_s)
+
+    for load in [load_lat, load_wi, load_gain, load_qkv, *load_o, load_lens, load_fgain, load_ho]:
+        load.start()
 
     flip = reversal().astype(BF)
     load_lat.wait()
@@ -173,7 +176,29 @@
         turned = jnp.where(low, rows.astype(F32), dot(flip, rows))
         lat_send[a] = packed(turned).astype(BF)
 
-    n_greet = 17 + jnp.where(low, 8, 0) + jnp.where(y == 1, 8, 0) + core
+    def fold_weights():
+        load_wi.wait()
+        load_gain.wait()
+        wi = wi_ref[...].astype(F32)
+        centred = wi - jnp.mean(wi, axis=1, keepdims=True)
+        wg_hi, wg_lo = hi_lo(centred * gain_ref[...].reshape(1, -1))
+        wg = jnp.concatenate([wg_hi, wg_lo], axis=0)
+        load_qkv.wait()
+        fold2 = dot_nt(qkv_v[...].reshape(192, -1), wg)
+        fold = fold2[:, :64] + fold2[:, 64:]
+        fold_buf[me, 0:64] = jnp.concatenate([fold[:64], fold[64:128]], axis=1).astype(BF)
+        fold_buf[me, 64:96] = packed(fold[128:].T).astype(BF)
+
+        c_hi, c_lo = hi_lo(centred)
+        cc = jnp.concatenate([c_hi, c_lo], axis=0)
+        gram4 = dot_nt(cc, cc)
+        gram2 = gram4[:64] + gram4[64:]
+        gram_hi, gram_lo = hi_lo((gram2[:, :64] + gram2[:, 64:]) * (1.0 / wi.shape[1]))
+        gram_buf[...] = jnp.concatenate([gram_hi, gram_lo], axis=0)
+
+    fold_weights()
+
+    n_greet = 18 + jnp.where(low, 1, 0) + y + core
     pl.semaphore_wait(barrier, n_greet)
 
     def lat_copy(src, dst, ssem, rsem, gg, ss):
@@ -186,67 +211,44 @@
             device_id_type=MESH,
         )
 
+    main_at = jnp.where(low, s, 23 - s)
+
     def lat_sends(act):
         @pl.loop(0, 8)
         def _(j):
             k = (z + j + 4) % 8
-            near = j == 4
-
-            @pl.when(low)
-            def _():
-                @pl.when(jnp.logical_not(jnp.logical_and(near, y == 0)))
-                def _():
-                    act(lat_copy(lat_send, lat_ht.at[s], lat_ssem.at[0, k], s, g, 2 * k))
-
-                @pl.when(jnp.logical_not(jnp.logical_and(near, y == 1)))
+            for a in range(2):
+
+                @pl.when(jnp.logical_not(jnp.logical_and(j == 4, y == a)))
                 def _():
                     act(
                         lat_copy(
-                            lat_send.at[1], lat_ht.at[s, 0], lat_ssem.at[1, k], s, g, 2 * k + 1
+                            lat_send.at[a],
+                            lat_tok.at[main_at],
+                            lat_ssem.at[a, k],
+                            main_at,
+                            g,
+                            2 * k + a,
                         )
                     )
 
-                act(
-                    lat_copy(
-                        lat_send.at[0],
-                        lat_ht.at[s, 1],
-                        lat_ssem.at[2, k],
-                        8 + s,
-                        prev_g,
-                        2 * k + 1,
-                    )
-                )
-
-            @pl.when(jnp.logical_not(low))
-            def _():
-                for a in range(2):
-
-                    @pl.when(jnp.logical_not(jnp.logical_and(near, y == a)))
-                    def _():
-                        act(
-                            lat_copy(
-                                lat_send.at[a],
-                                lat_r.at[15 - s],
-                                lat_ssem.at[a, k],
-                                31 - s,
-                                g,
-                                2 * k + a,
-                            )
-                        )
-
-    lat_sends(lambda c: c.start())
-
-    @pl.when(jnp.logical_and(low, y == 0))
+    lat_early = [
+        lat_copy(
+            lat_send.at[1 - a],
+            lat_next.at[a],
+            lat_ssem.at[2, a],
+            16 + a,
+            g if a == 0 else prev_g,
+            15 - s,
+        )
+        for a in range(2)
+    ]
+
+    @pl.when(low)
     def _():
-        lat_ht[s] = lat_send[...]
-
-    @pl.when(jnp.logical_and(low, y == 1))
-    def _():
-        lat_ht[s, 0] = lat_send[1]
-
-    @pl.when(jnp.logical_not(low))
-    def _():
-        lat_r[15 - s] = lat_send[y]
+        for early in lat_early:
+            early.start()
+        lat_sends(lambda c: c.start())
 
     def o_copy(part, block, ssem, gg, ss):
         return pltpu.make_async_remote_copy(
@@ -287,18 +289,6 @@
 
     def arrived(part, block):
         o_copy(part, block, z_ssem.at[0], sib_g, s).wait_recv()
-
-    load_wi.wait()
-    load_gain.wait()
-    wi = wi_ref[...].astype(F32)
-    centred = wi - jnp.mean(wi, axis=1, keepdims=True)
-    wg_hi, wg_lo = hi_lo(centred * gain_ref[...].reshape(1, -1))
-    wg = jnp.concatenate([wg_hi, wg_lo], axis=0)
-    load_qkv.wait()
-    fold2 = dot_nt(qkv_v[...].reshape(192, -1), wg)
-    fold = fold2[:, :64] + fold2[:, 64:]
-    fold_buf[me, 0:64] = jnp.concatenate([fold[:64], fold[64:128]], axis=1).astype(BF)
-    fold_buf[me, 64:96] = packed(fold[128:].T).astype(BF)
 
     def fold_copy(part, block, ssem, gg, ss):
         rows = pl.ds(pl.multiple_of(part * 48, 16), 48)
@@ -333,52 +323,105 @@
         first.start()
     across(me).start()
 
-    c_hi, c_lo = hi_lo(centred)
-    cc = jnp.concatenate([c_hi, c_lo], axis=0)
-    gram4 = dot_nt(cc, cc)
-    gram2 = gram4[:64] + gram4[64:]
-    gram = (gram2[:, :64] + gram2[:, 64:]) * (1.0 / wi.shape[1])
-    gram_hi, gram_lo = hi_lo(gram)
-    gram_st = jnp.concatenate([gram_hi, gram_lo], axis=0)
+    load_lens.wait()
+
+    def length(node):
+        last = lens_ref.shape[0] - 1
+        return jnp.where(node <= last, lens_ref[jnp.minimum(node, last)], 0)
+
+    @pl.when(jnp.logical_not(low))
+    def _():
+        row = lax.broadcasted_iota(jnp.int32, (PACK, 128), 0)
+        col = lax.broadcasted_iota(jnp.int32, (PACK, 128), 1)
+        at = 64 * (15 - s) + row + 32 * (col // 64)
+        for a in range(2):
+            lat_early[a].wait_recv()
+            lat_send[a] = jnp.where(
+                at < length(2 * g + a), lat_next[a].astype(F32), lat_send[a].astype(F32)
+            ).astype(BF)
+        lat_sends(lambda c: c.start())
+
+    lat_tok[main_at] = lat_send[y]
 
     def variance(xt):
-        gx = dot(gram_st, xt.astype(BF))
+        gx = dot(gram_buf[...], xt.astype(BF))
         return jnp.maximum(jnp.sum((gx[:64] + gx[64:]) * xt, axis=0, keepdims=True), 0.0)
 
-    load_lens.wait()
-    node = 2 * g + y
-    tail_len = jnp.where(node < lens_ref.shape[0], lens_ref[jnp.minimum(node, lens_ref.shape[0] - 1)], 0)
-
-    def lat_arrived(dst, rsem):
-        lat_copy(dst, dst, lat_ssem.at[0, 0], rsem, sib_g, s).wait_recv()
-
-    @pl.loop(0, 8)
+    tail_len = length(2 * g + y)
+
+    def at_step(n):
+        turn = n % 4
+        near = (z // 2 + jnp.where(turn < 2, turn, 5 - turn)) % 4
+        return 8 * jnp.where(n < 4, y, 1 - y) + 2 * near
+
+    def fold_relay(n):
+        for h in range(2):
+            block = at_step(n) + h
+
+            @pl.when(block != me)
+            def _():
+                fold_arrived(core, block)
+
+                @pl.when(n < 4)
+                def _():
+                    fold_across(block).start()
+
+                fold_sib(block).start()
+
+    def around(d, of):
+        return [
+            (of(d), d >= 0),
+            (of(-d), jnp.logical_and(d != 0, d != 4)),
+        ]
+
+    def pass_on_z(i):
+        d = jnp.where(i == 0, 2, jnp.where(i == 1, 1, i + 1))
+        for block, there in around(d, column):
+
+            @pl.when(there)
+            def _():
+                arrived(mine, block)
+                across(block).start()
+                to_x(block).start()
+                to_sib(mine, block).start()
+
+        @pl.when(i == 0)
+        def _():
+            on_up.start()
+            on_down.start()
+            on_far.start()
+
+    def pass_on_y(i):
+        d = jnp.where(i == 1, 2, jnp.where(i == 2, 1, i))
+        for block, there in around(d, other):
+
+            @pl.when(there)
+            def _():
+                arrived(mine, block)
+                to_x(block).start()
+                to_sib(mine, block).start()
+
+    theirs = 2 * (1 - px) + core
+
+    def pass_on_x(d, of):
+        for block, there in around(d, of):
+
+            @pl.when(there)
+            def _():
+                arrived(theirs, block)
+                to_sib(theirs, block).start()
+
+    for n in range(4):
+        fold_relay(jnp.int32(n))
+
+    @pl.loop(0, 16)
     def _(k):
-        @pl.when(jnp.logical_and(y == 0, k != s))
-        def _():
-            lat_arrived(lat_ht.at[k], k)
-
-        @pl.when(y == 1)
-        def _():
-            @pl.when(k != s)
-            def _():
-                lat_arrived(lat_ht.at[k, 0], k)
-
-            lat_arrived(lat_ht.at[k, 1], 8 + k)
-
-        @pl.when(15 - k != s)
-        def _():
-            lat_arrived(lat_r.at[k], 16 + k)
-
-    line = lax.broadcasted_iota(jnp.int32, (256, 128), 0)
-    lane = lax.broadcasted_iota(jnp.int32, (256, 128), 1)
-    spot = 64 * (line // 32) + line % 32 + 32 * (lane // 64)
-    head_lines = lat_ht[:, 0].astype(F32).reshape(256, 128)
-    tail_lines = jnp.where(
-        spot < tail_len,
-        lat_ht[:, 1].astype(F32).reshape(256, 128),
-        lat_r[...].astype(F32).reshape(256, 128),
-    )
+        @pl.when(k != main_at)
+        def _():
+            lat_copy(lat_send.at[0], lat_tok.at[k], lat_ssem.at[0, 0], k, sib_g, s).wait_recv()
+
+    head_lines = lat_tok[0:8].astype(F32).reshape(256, 128)
+    tail_lines = lat_tok[8:16].astype(F32).reshape(256, 128)
     tokens = jnp.concatenate([unpacked(head_lines), unpacked(tail_lines)], axis=0)
     xt = tokens.T
     xkt[0:64, :] = jnp.zeros((64, 1024), BF)
@@ -394,11 +437,8 @@
     w_tail[:, :128] = w[512:].astype(BF)
     w_tail[:, 128:] = jnp.where(tail_spot < tail_len, w[512:], 0.0).astype(BF)
 
-    q_line = lax.broadcasted_iota(jnp.int32, (32, 128), 0)
-    q_lane = lax.broadcasted_iota(jnp.int32, (32, 128), 1)
-    q_spot = 64 * tail_block + q_line + 32 * (q_lane // 64)
-    q_tail = jnp.where(q_spot < tail_len, lat_ht[tail_block, 1].astype(F32), lat_r[tail_block].astype(F32))
-    q_tok = jnp.concatenate([unpacked(lat_ht[head_block, 0].astype(F32)), unpacked(q_tail)], axis=0)
+    q_tail = lat_tok[8 + tail_block].astype(F32)
+    q_tok = jnp.concatenate([unpacked(lat_tok[head_block].astype(F32)), unpacked(q_tail)], axis=0)
     q_xt = q_tok.T
     q_eps = 1e-6 * (variance(q_xt) + 1e-5)
     q_xtz = jnp.concatenate([q_xt.astype(BF), jnp.zeros((64, 128), BF)], axis=0)
@@ -412,76 +452,12 @@
             parts.append(rows * (lax.rsqrt(mean + eps) * scale))
         return jnp.concatenate(parts, axis=0)
 
-    def at_step(n):
-        turn = n % 4
-        near = (z // 2 + jnp.where(turn < 2, turn, 5 - turn)) % 4
-        return 8 * jnp.where(n < 4, y, 1 - y) + 2 * near
-
-    def fold_relay(n):
-        for h in range(2):
-            block = at_step(n) + h
-
-            @pl.when(block != me)
-            def _():
-                fold_arrived(core, block)
-
-                @pl.when(n < 4)
-                def _():
-                    fold_across(block).start()
-
-                fold_sib(block).start()
-
-    def around(d, of):
-        return [
-            (of(d), d >= 0),
-            (of(-d), jnp.logical_and(d != 0, d != 4)),
-        ]
-
-    def pass_on_z(i):
-        d = jnp.where(i == 0, 2, jnp.where(i == 1, 1, i + 1))
-        for block, there in around(d, column):
-
-            @pl.when(there)
-            def _():
-                arrived(mine, block)
-                across(block).start()
-                to_x(block).start()
-                to_sib(mine, block).start()
-
-        @pl.when(i == 0)
-        def _():
-            on_up.start()
-            on_down.start()
-            on_far.start()
-
-    def pass_on_y(i):
-        d = jnp.where(i == 1, 2, jnp.where(i == 2, 1, i))
-        for block, there in around(d, other):
-
-            @pl.when(there)
-            def _():
-                arrived(mine, block)
-                to_x(block).start()
-                to_sib(mine, block).start()
-
-    theirs = 2 * (1 - px) + core
-
-    def pass_on_x(d, of):
-        for block, there in around(d, of):
-
-            @pl.when(there)
-            def _():
-                arrived(theirs, block)
-                to_sib(theirs, block).start()
-
-    fold_relay(0)
-    fold_relay(1)
 
     @pl.loop(0, 8)
     def _(n):
-        @pl.when(n < 6)
-        def _():
-            fold_relay(n + 2)
+        @pl.when(n < 4)
+        def _():
+            fold_relay(n + 4)
 
         first = at_step(n)
         for h in range(2):
@@ -525,22 +501,26 @@
             i = n - 3
             pass_on_x(jnp.where(i == 0, 2, jnp.where(i == 1, 1, i + 1)), column)
 
+
+    tok2 = jnp.concatenate([q_tok, q_tok[64:]], axis=0).astype(BF)
+    def project(part):
+        columns = pl.ds(pl.multiple_of(part * quarter, 128), quarter)
+        mix[:, columns] = dot(att[...], o_buf[part]) + dot(tok2, wi_ref[:, columns])
+
+    def from_sib(part):
+        @pl.loop(1, 16)
+        def _(k):
+            arrived(part, (me + k) % 16)
+
+    project(mine)
+    from_sib(2 * px + 1 - core)
+    project(2 * px + 1 - core)
     for d in (0, 2, 1, 3, 4):
         pass_on_x(jnp.int32(d), other)
-
-    @pl.loop(1, 16)
-    def _(k):
-        for half in range(2):
-            arrived(2 * half + 1 - core, (me + k) % 16)
-
-    tok2 = jnp.concatenate([q_tok, q_tok[64:]], axis=0).astype(BF)
-    mixed = jnp.concatenate(
-        [
-            dot(att[...], o_buf[k]) + dot(tok2, wi_ref[:, k * quarter : (k + 1) * quarter])
-            for k in range(4)
-        ],
-        axis=1,
-    )
+    project(theirs)
+    from_sib(2 * (1 - px) + 1 - core)
+    project(2 * (1 - px) + 1 - core)
+    mixed = mix[...]
     mean = jnp.mean(mixed, axis=1, keepdims=True)
     centre = mixed - mean
     spread = jnp.mean(centre * centre, axis=1, keepdims=True)
@@ -586,34 +566,12 @@
         def _():
             sc_recv[at] = sc_send[k]
 
-    @pl.when(jnp.logical_not(low))
-    def _():
-        sc_recv[2] = jnp.zeros((PACK, 128), F32)
-        sc_recv[3] = jnp.zeros((PACK, 128), F32)
-
-    kept = jnp.logical_or(own[0], own[2])
-    for a in range(2):
-
-        @pl.when(jnp.logical_not(jnp.logical_and(kept, y == a)))
-        def _():
-            sc_copy(0, g, s, a).wait_recv()
+    lat_sends(lambda c: c.wait_send())
 
     @pl.when(low)
     def _():
-        sc_copy(0, g, s, 2).wait_recv()
-
-        @pl.when(jnp.logical_not(own[1]))
-        def _():
-            sc_copy(0, g, s, 3).wait_recv()
-
-    row = 64 * s + lax.broadcasted_iota(jnp.int32, (64, 64), 0)
-    for a in range(2):
-        slot = 2 * g + a
-        gone = jnp.where(slot < lens_ref.shape[0], lens_ref[jnp.minimum(slot, lens_ref.shape[0] - 1)], 0)
-        step = lat_ref[a] + STEP * unpacked(sc_recv[a] + sc_recv[2 + a])
-        out_ref[a] = jnp.where(row < 1024 - gone, step, 0.0)
-
-    lat_sends(lambda c: c.wait_send())
+        for early in lat_early:
+            early.wait_send()
 
     @pl.loop(1, 16)
     def _(k):
@@ -634,6 +592,33 @@
     def _(k):
         across(8 * y + k).wait_send()
         fold_across(8 * y + k).wait_send()
+
+    @pl.when(jnp.logical_not(low))
+    def _():
+        sc_recv[2] = jnp.zeros((PACK, 128), F32)
+        sc_recv[3] = jnp.zeros((PACK, 128), F32)
+
+    kept = jnp.logical_or(own[0], own[2])
+    for a in range(2):
+
+        @pl.when(jnp.logical_not(jnp.logical_and(kept, y == a)))
+        def _():
+            sc_copy(0, g, s, a).wait_recv()
+
+    @pl.when(low)
+    def _():
+        sc_copy(0, g, s, 2).wait_recv()
+
+        @pl.when(jnp.logical_not(own[1]))
+        def _():
+            sc_copy(0, g, s, 3).wait_recv()
+
+    row = 64 * s + lax.broadcasted_iota(jnp.int32, (64, 64), 0)
+    for a in range(2):
+        slot = 2 * g + a
+        gone = length(slot)
+        step = lat_ref[a] + STEP * unpacked(sc_recv[a] + sc_recv[2 + a])
+        out_ref[a] = jnp.where(row < 1024 - gone, step, 0.0)
 
     for k in range(3):
 
@@ -664,14 +649,16 @@
                 pltpu.VMEM((width,), F32),
                 pltpu.VMEM(head_out.shape[::-1], BF),
                 pltpu.VMEM((2, PACK, 128), BF),
-                pltpu.VMEM((8, 2, PACK, 128), BF),
-                pltpu.VMEM((8, PACK, 128), BF),
+                pltpu.VMEM((16, PACK, 128), BF),
+                pltpu.VMEM((2, PACK, 128), BF),
                 pltpu.VMEM((16, 96, 128), BF),
+                pltpu.VMEM((128, HDIM), BF),
                 pltpu.VMEM((4, 1024, width // 4), BF),
                 pltpu.VMEM((128, 1024), BF),
                 pltpu.VMEM((512, 128), BF),
                 pltpu.VMEM((512, 256), BF),
                 pltpu.VMEM((192, 1024), BF),
+                pltpu.VMEM((192, width), F32),
                 pltpu.VMEM((3, PACK, 128), F32),
                 pltpu.VMEM((4, PACK, 128), F32),
                 dma((7,)),

time: 48.9 us -> 47.2 us (0.965)
  the two profiles are of different devices: /device:TPU:8 before, /device:TPU:40 now
where the time goes in v4:
time: 47.2 us; the launch traced here: 47.1 us
  Pallas kernels  45.6 us (97%)
  local copies, waits for them, and re-layouts  1.47 us (3%)
    pallas_call x1, Pallas kernels, body(): pl.pallas_call(functools.partial(kernel, groups), out_shape=jax.ShapeDtyp...  45.6 us
    unnamed x1, local copies, waits for them, and re-layouts  1.47 us

profile of v4, /device:TPU:40, one launch (start us, length us, event | category | flops | bytes accessed | tf_op | source)
XLA Modules:
  0.0 47.1 jit_solution(4620835283623780192)
XLA Ops:
  0.0 45.6 %shard_map.82 = f32[2,64,64]{2,1,0:T(8,128)} custom-call(f32[2,64,64]{2,1,0:T(8,128)} %lat_hbm.1, s32[31]{0:T(128)} %lens_hbm.1, bf16[64,1536]{1,0:T(8,128)(2,1)} %wi_hbm.1, f32[1536]{0:T(1024)} %gain_hbm.1, bf16[3,64,1536]{2,1,0:T(8,128)(2,1)} %bitcast.2, bf16[64,1536]{1,0:T(8,128)(2,1)} %o_hbm.1, f32[1536]{0:T(1024)} %fgain_hbm.1, bf16[64,1536]{1,0:T(8,128)(2,1)} %bitcast.3), custom_call_target="tpu_custom_call" | custom-call | tf_op jit(solution)/shard_map/pallas_call | solution.py:638
  45.6 1.5 %copy.10 = f32[2,64,64]{2,1,0:T(8,128)} copy(f32[2,64,64]{2,1,0:T(8,128)} %shard_map.82) | data formatting | bytes 65536

commit v5 on v4

--- a/solution.py
+++ b/solution.py
@@ -75,6 +75,8 @@
     w_tail,
     att,
     mix,
+    key_buf,
+    query_buf,
     sc_send,
     sc_recv,
     load_sem,
@@ -413,6 +415,8 @@
 
     for n in range(4):
         fold_relay(jnp.int32(n))
+    pass_on_z(jnp.int32(0))
+    pass_on_z(jnp.int32(1))
 
     @pl.loop(0, 16)
     def _(k):
@@ -453,26 +457,43 @@
         return jnp.concatenate(parts, axis=0)
 
 
+    def prepare(n):
+        first = at_step(n)
+        for h in range(2):
+
+            @pl.when(first + h != me)
+            def _():
+                fold_arrived(1 - core, first + h)
+
+    def keys_of(n, turn):
+        pair = fold_buf[pl.ds(at_step(n), 2), 0:64]
+        pair_qk = jnp.concatenate([pair[0], pair[1]], axis=0)
+        key_buf[turn] = rms(dot(pair_qk, xkt[...]), key_eps, 1.0).astype(BF)
+        query = rms(dot(pair_qk, q_xtz), q_eps, QSCALE).T
+        query_buf[turn] = jnp.concatenate(
+            [jnp.where(q_side, query, 0.0), jnp.where(q_side, 0.0, query)], axis=0
+        ).astype(BF)
+
+    prepare(jnp.int32(0))
+    keys_of(jnp.int32(0), 0)
+
     @pl.loop(0, 8)
     def _(n):
         @pl.when(n < 4)
         def _():
             fold_relay(n + 4)
 
+        later = jnp.minimum(n + 1, 7)
+
+        @pl.when(n < 7)
+        def _():
+            prepare(later)
+
         first = at_step(n)
-        for h in range(2):
-
-            @pl.when(first + h != me)
-            def _():
-                fold_arrived(1 - core, first + h)
-
         pair = fold_buf[pl.ds(first, 2)]
-        pair_qk = jnp.concatenate([pair[0, :64], pair[1, :64]], axis=0)
-        keys_t = rms(dot(pair_qk, xkt[...]), key_eps, 1.0).astype(BF)
-        query = rms(dot(pair_qk, q_xtz), q_eps, QSCALE).T
-        query2 = jnp.concatenate(
-            [jnp.where(q_side, query, 0.0), jnp.where(q_side, 0.0, query)], axis=0
-        ).astype(BF)
+        query2 = query_buf[n % 2]
+        keys_t = key_buf[n % 2]
+        keys_of(later, (n + 1) % 2)
         p = jnp.exp2(dot(query2, keys_t)).astype(BF)
         u_head = dot(p[:, :512], w_head[...])
         u_tail = dot(p[:, 512:], w_tail[...])
@@ -488,17 +509,17 @@
         columns = pl.ds(pl.multiple_of(first * 64, 128), 128)
         att[:, columns] = jnp.concatenate([att_even, att_odd], axis=1).astype(BF)
 
-        @pl.when(n < 4)
-        def _():
-            pass_on_z(n)
-
-        @pl.when(jnp.logical_and(n >= 1, n < 6))
-        def _():
-            pass_on_y(n - 1)
-
-        @pl.when(jnp.logical_and(n >= 3, n < 7))
-        def _():
-            i = n - 3
+        @pl.when(n < 2)
+        def _():
+            pass_on_z(n + 2)
+
+        @pl.when(n < 5)
+        def _():
+            pass_on_y(n)
+
+        @pl.when(jnp.logical_and(n >= 2, n < 6))
+        def _():
+            i = n - 2
             pass_on_x(jnp.where(i == 0, 2, jnp.where(i == 1, 1, i + 1)), column)
 
 
@@ -659,6 +680,8 @@
                 pltpu.VMEM((512, 256), BF),
                 pltpu.VMEM((192, 1024), BF),
                 pltpu.VMEM((192, width), F32),
+                pltpu.VMEM((2, 128, 1024), BF),
+                pltpu.VMEM((2, 256, 128), BF),
                 pltpu.VMEM((3, PACK, 128), F32),
                 pltpu.VMEM((4, PACK, 128), F32),
                 dma((7,)),

time: 47.2 us -> 45.1 us (0.956)
  the two profiles are of different devices: /device:TPU:40 before, /device:TPU:8 now
where the time goes in v5:
time: 45.1 us; the launch traced here: 45 us
  Pallas kernels  43.5 us (96%)
  local copies, waits for them, and re-layouts  1.47 us (3%)
    pallas_call x1, Pallas kernels, body(): pl.pallas_call(functools.partial(kernel, groups), out_shape=jax.ShapeDtyp...  43.5 us
    unnamed x1, local copies, waits for them, and re-layouts  1.47 us

profile of v5, /device:TPU:8, one launch (start us, length us, event | category | flops | bytes accessed | tf_op | source)
XLA Modules:
  0.0 45.0 jit_solution(7978709082509168664)
XLA Ops:
  0.0 43.5 %shard_map.82 = f32[2,64,64]{2,1,0:T(8,128)} custom-call(f32[2,64,64]{2,1,0:T(8,128)} %lat_hbm.1, s32[31]{0:T(128)} %lens_hbm.1, bf16[64,1536]{1,0:T(8,128)(2,1)} %wi_hbm.1, f32[1536]{0:T(1024)} %gain_hbm.1, bf16[3,64,1536]{2,1,0:T(8,128)(2,1)} %bitcast.2, bf16[64,1536]{1,0:T(8,128)(2,1)} %o_hbm.1, f32[1536]{0:T(1024)} %fgain_hbm.1, bf16[64,1536]{1,0:T(8,128)(2,1)} %bitcast.3), custom_call_target="tpu_custom_call" | custom-call | tf_op jit(solution)/shard_map/pallas_call | solution.py:659
  43.5 1.5 %copy.10 = f32[2,64,64]{2,1,0:T(8,128)} copy(f32[2,64,64]{2,1,0:T(8,128)} %shard_map.82) | data formatting | bytes 65536

commit v6 on v5

--- a/solution.py
+++ b/solution.py
@@ -509,17 +509,17 @@
         columns = pl.ds(pl.multiple_of(first * 64, 128), 128)
         att[:, columns] = jnp.concatenate([att_even, att_odd], axis=1).astype(BF)
 
-        @pl.when(n < 2)
-        def _():
-            pass_on_z(n + 2)
-
-        @pl.when(n < 5)
-        def _():
-            pass_on_y(n)
-
-        @pl.when(jnp.logical_and(n >= 2, n < 6))
-        def _():
-            i = n - 2
+        @pl.when(jnp.logical_and(n >= 1, n < 3))
+        def _():
+            pass_on_z(n + 1)
+
+        @pl.when(jnp.logical_and(n >= 1, n < 6))
+        def _():
+            pass_on_y(n - 1)
+
+        @pl.when(jnp.logical_and(n >= 3, n < 7))
+        def _():
+            i = n - 3
             pass_on_x(jnp.where(i == 0, 2, jnp.where(i == 1, 1, i + 1)), column)
 
 

time: 45.1 us -> 44.4 us (0.984)
  Pallas kernels: 43.5 us -> 42.7 us
    pallas_call x1, Pallas kernels: 43.5 us -> 42.7 us  [body(): pl.pallas_call(functools.partial(kernel, groups), out_shape=jax.ShapeDtyp...]
where the time goes in v6:
time: 44.4 us; the launch traced here: 44.2 us
  Pallas kernels  42.7 us (96%)
  local copies, waits for them, and re-layouts  1.47 us (3%)
    pallas_call x1, Pallas kernels, body(): pl.pallas_call(functools.partial(kernel, groups), out_shape=jax.ShapeDtyp...  42.7 us
    unnamed x1, local copies, waits for them, and re-layouts  1.47 us

profile of v6, /device:TPU:8, one launch (start us, length us, event | category | flops | bytes accessed | tf_op | source)
XLA Modules:
  0.0 44.2 jit_solution(6329176180235974443)
XLA Ops:
  0.0 42.7 %shard_map.82 = f32[2,64,64]{2,1,0:T(8,128)} custom-call(f32[2,64,64]{2,1,0:T(8,128)} %lat_hbm.1, s32[31]{0:T(128)} %lens_hbm.1, bf16[64,1536]{1,0:T(8,128)(2,1)} %wi_hbm.1, f32[1536]{0:T(1024)} %gain_hbm.1, bf16[3,64,1536]{2,1,0:T(8,128)(2,1)} %bitcast.2, bf16[64,1536]{1,0:T(8,128)(2,1)} %o_hbm.1, f32[1536]{0:T(1024)} %fgain_hbm.1, bf16[64,1536]{1,0:T(8,128)(2,1)} %bitcast.3), custom_call_target="tpu_custom_call" | custom-call | tf_op jit(solution)/shard_map/pallas_call | solution.py:659
  42.7 1.5 %copy.10 = f32[2,64,64]{2,1,0:T(8,128)} copy(f32[2,64,64]{2,1,0:T(8,128)} %shard_map.82) | data formatting | bytes 65536

commit v7 on v6

--- a/solution.py
+++ b/solution.py
@@ -533,11 +533,11 @@
         def _(k):
             arrived(part, (me + k) % 16)
 
+    for d in (0, 2, 1, 3, 4):
+        pass_on_x(jnp.int32(d), other)
     project(mine)
     from_sib(2 * px + 1 - core)
     project(2 * px + 1 - core)
-    for d in (0, 2, 1, 3, 4):
-        pass_on_x(jnp.int32(d), other)
     project(theirs)
     from_sib(2 * (1 - px) + 1 - core)
     project(2 * (1 - px) + 1 - core)

time: 44.4 us -> 43.9 us (0.989)
    pallas_call x1, Pallas kernels: 42.7 us -> 42.3 us  [body(): pl.pallas_call(functools.partial(kernel, groups), out_shape=jax.ShapeDtyp...]
where the time goes in v7:
time: 43.9 us; the launch traced here: 43.8 us
  Pallas kernels  42.3 us (96%)
  local copies, waits for them, and re-layouts  1.47 us (3%)
    pallas_call x1, Pallas kernels, body(): pl.pallas_call(functools.partial(kernel, groups), out_shape=jax.ShapeDtyp...  42.3 us
    unnamed x1, local copies, waits for them, and re-layouts  1.47 us

profile of v7, /device:TPU:8, one launch (start us, length us, event | category | flops | bytes accessed | tf_op | source)
XLA Modules:
  0.0 43.8 jit_solution(11655952953676981834)
XLA Ops:
  0.0 42.3 %shard_map.82 = f32[2,64,64]{2,1,0:T(8,128)} custom-call(f32[2,64,64]{2,1,0:T(8,128)} %lat_hbm.1, s32[31]{0:T(128)} %lens_hbm.1, bf16[64,1536]{1,0:T(8,128)(2,1)} %wi_hbm.1, f32[1536]{0:T(1024)} %gain_hbm.1, bf16[3,64,1536]{2,1,0:T(8,128)(2,1)} %bitcast.2, bf16[64,1536]{1,0:T(8,128)(2,1)} %o_hbm.1, f32[1536]{0:T(1024)} %fgain_hbm.1, bf16[64,1536]{1,0:T(8,128)(2,1)} %bitcast.3), custom_call_target="tpu_custom_call" | custom-call | tf_op jit(solution)/shard_map/pallas_call | solution.py:659
  42.3 1.5 %copy.10 = f32[2,64,64]{2,1,0:T(8,128)} copy(f32[2,64,64]{2,1,0:T(8,128)} %shard_map.82) | data formatting | bytes 65536

commit v8 on v7

--- a/solution.py
+++ b/solution.py
@@ -554,14 +554,6 @@
     counted = where_t < tail_len
     sc_send[0] = packed(score[:64])
     sc_send[1] = packed(jnp.where(counted, score[64:128] - score[128:], 0.0))
-    turned = jnp.dot(
-        reversal(),
-        jnp.where(counted, 0.0, score[64:128]),
-        precision=lax.Precision.HIGHEST,
-        preferred_element_type=F32,
-    )
-    sc_send[2] = packed(turned)
-
     tail_g = jnp.where(y == 0, g, next_g)
     targets = [(g, head_block, y), (tail_g, tail_block, 3 - y), (g, 15 - tail_block, y)]
 
@@ -578,6 +570,15 @@
     own = [s == head_block, jnp.logical_and(y == 0, s == tail_block), s == 15 - tail_block]
 
     for k, (gg, ss, at) in enumerate(targets):
+        if k == 2:
+            turned = jnp.dot(
+                reversal(),
+                jnp.where(counted, 0.0, score[64:128]),
+                precision=lax.Precision.HIGHEST,
+                preferred_element_type=F32,
+            )
+            sc_send[2] = packed(turned)
+
 
         @pl.when(jnp.logical_not(own[k]))
         def _():

time: 43.9 us -> 43.7 us (level)
  no operation moved by 1% of the time
where the time goes in v8:
time: 43.7 us; the launch traced here: 43.6 us
  Pallas kernels  42.1 us (96%)
  local copies, waits for them, and re-layouts  1.47 us (3%)
    pallas_call x1, Pallas kernels, body(): pl.pallas_call(functools.partial(kernel, groups), out_shape=jax.ShapeDtyp...  42.1 us
    unnamed x1, local copies, waits for them, and re-layouts  1.47 us

profile of v8, /device:TPU:8, one launch (start us, length us, event | category | flops | bytes accessed | tf_op | source)
XLA Modules:
  0.0 43.6 jit_solution(3492390756409334837)
XLA Ops:
  0.0 42.1 %shard_map.82 = f32[2,64,64]{2,1,0:T(8,128)} custom-call(f32[2,64,64]{2,1,0:T(8,128)} %lat_hbm.1, s32[31]{0:T(128)} %lens_hbm.1, bf16[64,1536]{1,0:T(8,128)(2,1)} %wi_hbm.1, f32[1536]{0:T(1024)} %gain_hbm.1, bf16[3,64,1536]{2,1,0:T(8,128)(2,1)} %bitcast.2, bf16[64,1536]{1,0:T(8,128)(2,1)} %o_hbm.1, f32[1536]{0:T(1024)} %fgain_hbm.1, bf16[64,1536]{1,0:T(8,128)(2,1)} %bitcast.3), custom_call_target="tpu_custom_call" | custom-call | tf_op jit(solution)/shard_map/pallas_call | solution.py:660
  42.1 1.5 %copy.10 = f32[2,64,64]{2,1,0:T(8,128)} copy(f32[2,64,64]{2,1,0:T(8,128)} %shard_map.82) | data formatting | bytes 65536
